TPU v7x, 128 devices: a whole 4x4x4 slice. The times are simulated.
128 devices in a mesh: gx: 4 (over z_hi, core), gy: 4 (over x), gz: 8 (over y, z_lo).
Axes of the slice: x: 4, y: 4, z: 4 (z_hi: 2, z_lo: 2; z = z_hi * 2 + z_lo), core: 2. Of those that a mesh axis runs over, the one named last changes fastest.
Arguments:
- offsets: float32 [16, 16, 16, 3, 16], P('gx', 'gy', 'gz'), as said below
- species: int32 [16, 16, 16, 16], P('gx', 'gy', 'gz'), may hold values from 0 to 3
- neighbours: int32 [16, 16, 16, 16, 32], P('gx', 'gy', 'gz'), may hold values from 0 to 6143
- counts: int32 [16, 16, 16, 16], P('gx', 'gy', 'gz'), may hold values from 8 to 32, as said below
- embed: float32 [4, 128], replicated, may hold values from 0.25 to 1.75
- radial_a: float32 [8, 128], replicated, may hold values from -2 to 2
- mix_in: bfloat16 [384, 128], replicated, may hold values from -0.3125 to 0.3125
- proj_center: bfloat16 [128, 128], replicated, may hold values from -0.5 to 0.5
- proj_neigh: bfloat16 [128, 128], replicated, may hold values from -0.5 to 0.5
- radial_b: float32 [8, 128], replicated, may hold values from -2 to 2
- couple: float32 [3, 128], replicated, may hold values from -4 to 4
- latent_two: bfloat16 [128, 128], replicated, may hold values from -0.5 to 0.5
- latent_three: bfloat16 [128, 128], replicated, may hold values from -0.5 to 0.5
- readout: float32 [128], replicated, may hold values from -0.5 to 0.5
Outputs:
- forces: float32 [16, 16, 16, 3, 16], P('gx', 'gy', 'gz')
- atom_energy: float32 [16, 16, 16, 16], P('gx', 'gy', 'gz')
Inputs may be any that keep to these rules, and one draw needn't show every extreme that they name: Slots 0 to count - 1 of an atom are live; the level of the counts differs from brick to brick, and the first atom of each brick has all 32. `offsets`: each atom lies within 0.1 of its own site in its cell: x at 0.5 + (slot % 2), y at 0.5 + (slot // 2 % 2), z at (slot // 4 + 0.5) * 8 / 16.
All inputs are finite; a program needn't handle non-finite values.
Results may differ from a plain program's by a relative error of at most 0.014.
Values may be sent and summed in bfloat16 or wider, within the bound.
No kernel may reach another device: no remote copies, remote signals or barrier semaphores. Data moves between devices by JAX's collectives and lax.ppermute only.
A program may use at most 128 MiB of HBM per device.

v0:
```python
import math

import jax
import jax.numpy as jnp
from jax import lax
from jax.experimental import pallas as pl
from jax.experimental.pallas import tpu as pltpu
from jax.sharding import PartitionSpec as P

CX = 4
CY = 4
CZ = 2
PER_CELL = 16
SLOTS = 32
CH = 128
NBASIS = 8
SPECIES = 4

CELL_SIDE = 2.0
CUTOFF = 10.5
NORM_EPS = 1e-05

COLS = CX * CY
PAIRS = CZ * PER_CELL * SLOTS
CELL_PAIRS = PER_CELL * SLOTS
ATOMS = COLS * CZ * PER_CELL
RUN = 48
SLAB = 5 * RUN
CELL_ROWS = 40
OWN_RUNS = CY * (CX + 4)
RIM_RUNS = 2 * (CX + 4)
LANES = PAIRS // 128

F32 = jnp.float32
BF16 = jnp.bfloat16
DEGREE = (0, 1, 1, 1, 2, 2, 2, 2, 2)

F_Y = 0
F_W = 9
F_DW = 10
F_B = 11
F_DB = 19
F_INV = 27
F_COUNT = 28

G_B = 0
G_Y = 8
G_E = 17
G_COUNT = 24


def dims(a, b, ca, cb):
    return lax.dot_general(a, b, (((ca,), (cb,)), ((), ())), preferred_element_type=F32)


def halves(value):
    high = value.astype(BF16)
    return high, (value - high.astype(F32)).astype(BF16)


def dims_three(a, b, ca, cb):
    a_high, a_low = halves(a)
    b_high, b_low = halves(b)
    return dims(a_high, b_high, ca, cb) + (
        dims(a_high, b_low, ca, cb) + dims(a_low, b_high, ca, cb)
    )


def iota(shape, dim):
    return lax.broadcasted_iota(jnp.int32, shape, dim)


def one_hot(condition):
    return jnp.where(condition, 1.0, 0.0).astype(BF16)


def hot_rows(count, code):
    rows = iota((count, PAIRS), 0).astype(F32).astype(BF16)
    return jnp.where(
        rows == code.astype(F32).astype(BF16), jnp.ones((), BF16), jnp.zeros((), BF16)
    )


def radial_blocks(radial):
    rows = []
    for m in range(9):
        before = [jnp.zeros((NBASIS, m * CH), F32)] if m else []
        after = [jnp.zeros((NBASIS, (8 - m) * CH), F32)] if m < 8 else []
        rows.append(jnp.concatenate(before + [radial] + after, 1))
    return jnp.concatenate(rows, 0)


def looped(count, body, group):
    def step(j, carry):
        running = [body(j * group + k, k) for k in range(group)]
        while running:
            running = [one for one in running if next(one, True) is None]
        return carry

    lax.fori_loop(0, count // group, step, 0)


def gated(half):
    t = jnp.tanh(half)
    up = t + 1.0
    act = half * up
    return act, up + act * (1.0 - t)


def sigmoid_of(v):
    return 0.5 * jnp.tanh(0.5 * v) + 0.5


def feature_rows(ref, row, count, i):
    blocks = []
    for lane in range(LANES):
        start = (lane * F_COUNT + row) * COLS + i
        blocks.append(ref[pl.ds(start, count, stride=COLS) if count > 1 else pl.ds(start, 1), :])
    return jnp.concatenate(blocks, 1)


def whole_feature(ref, row):
    blocks = []
    for lane in range(LANES):
        start = (lane * F_COUNT + row) * COLS
        blocks.append(ref[start : start + COLS, :])
    return jnp.concatenate(blocks, 1)


def put_feature(ref, row, value):
    for lane in range(LANES):
        start = (lane * F_COUNT + row) * COLS
        ref[start : start + COLS, :] = value[:, lane * 128 : (lane + 1) * 128]


def cell_window(ref, x, y):
    parts = []
    for dx in range(5):
        start = pl.multiple_of(((x + dx) * 8 + y) * 8, 8)
        parts.append(ref[pl.ds(start, CELL_ROWS), :])
    return jnp.concatenate(parts, 0)


def env_kernel(
    nbr_ref,
    ext_ref,
    own_ref,
    count_ref,
    species_ref,
    embed_ref,
    radial_ref,
    mix_ref,
    hidden_ref,
    env_ref,
    scale_ref,
    feat_ref,
    code_ref,
    near_ref,
    moment_ref,
):
    shape = (COLS, PAIRS)
    number = nbr_ref[...]
    slot = number & 15
    cell = number >> 4
    over = (cell * 43691) >> 18
    cell_z = cell - 6 * over
    cell_y = over & 7
    cell_x = over >> 3
    column = iota(shape, 0)
    lane = iota(shape, 1)
    dx = cell_x - (column >> 2)
    dy = cell_y - (column & 3)
    upper = (cell_z >= 3).astype(jnp.int32)
    code_ref[0] = (dy * 5 + dx) * RUN + (cell_z - 3 * upper) * PER_CELL + slot
    code_ref[1] = upper
    code_ref[2] = dx * CELL_ROWS + dy * 8 + cell_z
    code_ref[3] = slot

    row_slots = iota((PER_CELL, PAIRS), 0)

    def fetch(i, k):
        hot = hot_rows(5 * CELL_ROWS, code_ref[2, pl.ds(i, 1), :])
        high, low = halves(cell_window(ext_ref, i // CY, i % CY))
        places = dims(high, hot, 0, 0) + dims(low, hot, 0, 0)
        yield
        mask = row_slots == code_ref[3, pl.ds(i, 1), :]
        for c in range(3):
            part = places[c * PER_CELL : (c + 1) * PER_CELL]
            near_ref[c, pl.ds(i, 1), :] = jnp.sum(jnp.where(mask, part, 0.0), 0, keepdims=True)

    looped(COLS, fetch, 8)

    spread = one_hot(iota((32, PAIRS), 0) == (iota((32, PAIRS), 1) >> 5))
    own_high, own_low = halves(own_ref[...])
    own = dims(own_high, spread, 1, 0) + dims(own_low, spread, 1, 0)
    count = dims(count_ref[...].astype(F32).astype(BF16), spread, 1, 0)
    live = ((lane & 31).astype(F32) < count).astype(F32)
    step_x = (dx - 2).astype(F32) * CELL_SIDE + near_ref[0] - own[0:COLS]
    step_y = (dy - 2).astype(F32) * CELL_SIDE + near_ref[1] - own[COLS : 2 * COLS]
    step_z = (
        (cell_z - 2 - (lane >> 9)).astype(F32) * CELL_SIDE + near_ref[2] - own[2 * COLS : 3 * COLS]
    )
    square = step_x * step_x + step_y * step_y + step_z * step_z
    distance = jnp.sqrt(square)
    inverse = 1.0 / distance
    nx, ny, nz = step_x * inverse, step_y * inverse, step_z * inverse

    def put(row, value):
        put_feature(feat_ref, row, value)

    three, five, fifteen = math.sqrt(3.0), math.sqrt(5.0), math.sqrt(15.0)
    put(F_Y, jnp.ones(shape, F32))
    put(F_Y + 1, three * nx)
    put(F_Y + 2, three * ny)
    put(F_Y + 3, three * nz)
    put(F_Y + 4, fifteen * nx * ny)
    put(F_Y + 5, fifteen * ny * nz)
    put(F_Y + 6, (0.5 * five) * (3.0 * nz * nz - 1.0))
    put(F_Y + 7, fifteen * nx * nz)
    put(F_Y + 8, (0.5 * fifteen) * (nx * nx - ny * ny))
    scaled = distance * (1.0 / CUTOFF)
    inside = 1.0 - scaled * scaled
    put(F_W, live * inside * inside)
    put(F_DW, live * (-4.0 / CUTOFF) * scaled * inside)
    put(F_INV, inverse)
    angle = distance * (math.pi / CUTOFF)
    sine, cosine = jnp.sin(angle), jnp.cos(angle)
    last_s, last_c = jnp.zeros(shape, F32), jnp.ones(shape, F32)
    now_s, now_c = sine, cosine
    for k in range(1, NBASIS + 1):
        basis = CELL_SIDE * now_s * inverse
        put(F_B + k - 1, basis)
        put(F_DB + k - 1, (CELL_SIDE * k * math.pi / CUTOFF * now_c - basis) * inverse)
        last_s, now_s = now_s, 2.0 * cosine * now_s - last_s
        last_c, now_c = now_c, 2.0 * cosine * now_c - last_c

    atoms = one_hot(iota((PER_CELL, CELL_PAIRS), 0) == (iota((PER_CELL, CELL_PAIRS), 1) >> 5))

    def moments(i, k):
        harmonic = feature_rows(feat_ref, F_Y, 9, i)
        weighted = feature_rows(feat_ref, F_B, NBASIS, i) * feature_rows(feat_ref, F_W, 1, i)
        products = jnp.concatenate([harmonic[m : m + 1] * weighted for m in range(9)], 0)
        high, low = halves(products)
        yield
        for z in range(CZ):
            part = slice(z * CELL_PAIRS, (z + 1) * CELL_PAIRS)
            start = pl.multiple_of((i * CZ + z) * PER_CELL, PER_CELL)
            moment_ref[pl.ds(start, PER_CELL), :] = dims(atoms, high[:, part], 1, 1) + dims(
                atoms, low[:, part], 1, 1
            )

    looped(COLS, moments, 8)

    kind = one_hot(iota((SPECIES, ATOMS), 0) == species_ref[...])
    embed_high, embed_low = halves(embed_ref[...] * (1.0 / math.sqrt(SLOTS)))
    scale = dims(kind, embed_high, 0, 0) + dims(kind, embed_low, 0, 0)
    scale_ref[...] = scale
    sums = dims_three(moment_ref[...], radial_blocks(radial_ref[...]), 1, 0)
    invariants = [None] * 3
    for m in range(9):
        value = sums[:, m * CH : (m + 1) * CH] * scale
        env_ref[m] = value
        degree = DEGREE[m]
        squared = value * value
        invariants[degree] = (
            squared if invariants[degree] is None else invariants[degree] + squared
        )
    normed, _ = normalised(invariants)
    mixed = dims(jnp.concatenate(normed, 1).astype(BF16), mix_ref[...], 1, 0)
    hidden = (mixed * sigmoid_of(mixed)).astype(BF16)
    for y in range(CY):
        for x in range(CX):
            hidden_ref[y, x] = hidden[(x * CY + y) * 32 : (x * CY + y + 1) * 32]


def normalised(invariants):
    total = sum(jnp.sum(q * q, 1, keepdims=True) for q in invariants)
    inverse = lax.rsqrt(total * (1.0 / (3 * CH)) + NORM_EPS)
    return [q * inverse for q in invariants], inverse


def spans(z):
    return slice(z * CELL_PAIRS, (z + 1) * CELL_PAIRS)


def rows_of(column, z):
    return pl.ds(pl.multiple_of((column * CZ + z) * PER_CELL, PER_CELL), PER_CELL)


def slab_rows(block, x):
    return pl.ds(pl.multiple_of((block * 8 + x) * RUN, RUN), SLAB)


def fill_table(table_ref, start, around, weights, runs):
    for h in range(2):
        rows = around[:, h].reshape(runs * RUN, CH)
        table_ref[start : start + runs * RUN, h * CH : (h + 1) * CH] = dims(
            rows, weights, 1, 0
        ).astype(BF16) * jnp.asarray(0.5, BF16)


def atom_blocks():
    mask = iota((PER_CELL, CELL_PAIRS), 0) == (iota((PER_CELL, CELL_PAIRS), 1) >> 5)
    return mask, one_hot(mask)


def pair_features(harmonic, part, mask):
    return [jnp.where(mask, harmonic[m : m + 1, part], 0.0).astype(BF16) for m in range(9)]


def scaled_env(env_ref, couple, column, z):
    rows = rows_of(column, z)
    return [
        (env_ref[m, rows, :] * couple[DEGREE[m] : DEGREE[m] + 1]).astype(BF16)
        for m in range(9)
    ]


def early_kernel(
    around_ref,
    hidden_ref,
    env_ref,
    feat_ref,
    code_ref,
    center_ref,
    neigh_ref,
    radial_ref,
    couple_ref,
    early_ref,
    table_ref,
    own_ref,
):
    y = pl.program_id(0)

    @pl.when(y == 0)
    def _():
        fill_table(table_ref, 0, around_ref, neigh_ref[...], OWN_RUNS)
        for yy in range(CY):
            for x in range(CX):
                start = (x * CY + yy) * 32
                own_ref[start : start + 32, :] = dims(
                    hidden_ref[yy, x], center_ref[...], 1, 0
                ) * 0.5

    radial_high, radial_low = halves(radial_ref[...] * 0.5)
    couple = couple_ref[...] * 0.5
    mask, atoms = atom_blocks()

    def column(x, place, first, count, block):
        i = x * CY + y
        harmonic = feature_rows(feat_ref, F_Y, 9, i)
        basis_high, basis_low = halves(feature_rows(feat_ref, F_B, NBASIS, i))
        code = code_ref[0, pl.ds(i, 1), :]
        upper = code_ref[1, pl.ds(i, 1), :] > 0
        parts = []
        for z in range(CZ):
            part = spans(z)
            feature = jnp.concatenate(
                pair_features(harmonic, part, mask)
                + [
                    atoms,
                    atoms,
                    basis_high[:, part],
                    basis_low[:, part],
                    basis_high[:, part],
                    jnp.zeros((8, CELL_PAIRS), BF16),
                ],
                0,
            )
            own_high, own_low = halves(own_ref[rows_of(i, z), :])
            table = jnp.concatenate(
                scaled_env(env_ref, couple, i, z)
                + [
                    own_high,
                    own_low,
                    radial_high,
                    radial_high,
                    radial_low,
                    jnp.zeros((8, CH), BF16),
                ],
                0,
            )
            parts.append(dims(table, feature, 0, 0))
        yield
        fetched = None
        for k in range(count):
            hot = hot_rows(SLAB, code - (first + k) * SLAB)
            found = dims(table_ref[slab_rows(block + k, x), :], hot, 0, 0)
            fetched = found if fetched is None else fetched + found
        yield
        early_ref[x] = jnp.concatenate(parts, 1) + jnp.where(upper, fetched[CH:], fetched[:CH])

    @pl.when((y == 0) | (y == 3))
    def _():
        far = (y == 3).astype(jnp.int32)
        looped(CX, lambda x, k: column(x, k, 2 - 2 * far, 3, far), 4)

    @pl.when((y == 1) | (y == 2))
    def _():
        looped(CX, lambda x, k: column(x, k, 2 - y, 4, 0), 4)


def pair_kernel(
    early_ref,
    low_ref,
    up_ref,
    feat_ref,
    code_ref,
    neigh_ref,
    two_ref,
    three_ref,
    readout_ref,
    energy_ref,
    low_out_ref,
    up_out_ref,
    grad_ref,
    raw_ref,
    table_ref,
    total_ref,
    hot_ref,
):
    y = pl.program_id(0)

    @pl.when(y == 0)
    def _():
        fill_table(table_ref, 0, low_ref, neigh_ref[...], RIM_RUNS)
        fill_table(table_ref, RIM_RUNS * RUN, up_ref, neigh_ref[...], RIM_RUNS)
        total_ref[...] = jnp.zeros_like(total_ref)

    readout = jnp.transpose(jnp.broadcast_to(0.5 * readout_ref[...], (CH, CH)))
    readout = jnp.concatenate([readout] * LANES, 1)
    two_half = two_ref[...] * jnp.asarray(0.5, BF16)
    three_half = three_ref[...] * jnp.asarray(0.5, BF16)

    def column(x, place, first, count, block):
        i = x * CY + y
        weight = feature_rows(feat_ref, F_W, 1, i)
        code = code_ref[0, pl.ds(i, 1), :]
        upper = code_ref[1, pl.ds(i, 1), :] > 0
        fetched = None
        for k in range(count):
            hot = hot_rows(SLAB, code - (first + k) * SLAB)
            hot_ref[place, k * SLAB : (k + 1) * SLAB, :] = hot
            found = dims(table_ref[slab_rows(block + k, x), :], hot, 0, 0)
            fetched = found if fetched is None else fetched + found
        yield
        value = early_ref[x] + jnp.where(upper, fetched[CH:], fetched[:CH])
        one, slope_one = gated(value)
        value = dims(two_half, one.astype(BF16), 0, 0)
        yield
        two, slope_two = gated(value)
        value = dims(three_half, two.astype(BF16), 0, 0)
        yield
        top, slope_top = gated(value)
        raw_ref[pl.ds(i, 1), :] = 2.0 * jnp.sum(top * readout, 0, keepdims=True)
        grad = slope_top * (readout * weight)
        grad = dims(three_half, grad.astype(BF16), 1, 0)
        yield
        grad = dims(two_half, (grad * slope_two).astype(BF16), 1, 0)
        yield
        grad = grad * slope_one
        grad = grad.astype(BF16)
        high = grad * jnp.where(upper, 1.0, 0.0).astype(BF16)
        spread = jnp.concatenate([grad - high, high], 0)
        grad_ref[x] = grad
        found = dims(hot_ref[place, : count * SLAB, :], spread, 1, 1)
        yield
        for k in range(count):
            total_ref[slab_rows(block + k, x), :] += found[k * SLAB : (k + 1) * SLAB]

    @pl.when((y == 0) | (y == 3))
    def _():
        far = (y == 3).astype(jnp.int32)
        looped(CX, lambda x, k: column(x, k, 3 * far, 2, 2 * far), 4)

    @pl.when((y == 1) | (y == 2))
    def _():
        looped(CX, lambda x, k: column(x, k, 4 * (y - 1), 1, y), 4)

    @pl.when(y == CY - 1)
    def _():
        for h in range(2):
            rim = total_ref[:, h * CH : (h + 1) * CH].astype(BF16).reshape(2 * RIM_RUNS, RUN, CH)
            low_out_ref[:, h] = rim[:RIM_RUNS]
            up_out_ref[:, h] = rim[RIM_RUNS:]
        gather = one_hot(iota((32, PAIRS), 0) == (iota((32, PAIRS), 1) >> 5))
        high, low = halves(raw_ref[...] * whole_feature(feat_ref, F_W))
        energy_ref[...] = dims(high, gather, 1, 1) + dims(low, gather, 1, 1)


def spread_kernel(grad_ref, code_ref, ghost_ref, total_ref, hot_ref):
    y = pl.program_id(0)

    @pl.when(y == 0)
    def _():
        total_ref[...] = jnp.zeros_like(total_ref)


    def column(x, place, first, count, block):
        i = x * CY + y
        code = code_ref[0, pl.ds(i, 1), :]
        upper = jnp.where(code_ref[1, pl.ds(i, 1), :] > 0, 1.0, 0.0).astype(BF16)
        for k in range(count):
            hot_ref[place, k * SLAB : (k + 1) * SLAB, :] = hot_rows(
                SLAB, code - (first + k) * SLAB
            )
        grad = grad_ref[x]
        high = grad * upper
        spread = jnp.concatenate([grad - high, high], 0)
        found = dims(hot_ref[place, : count * SLAB, :], spread, 1, 1)
        for k in range(count):
            total_ref[slab_rows(block + k, x), :] += found[k * SLAB : (k + 1) * SLAB]
        yield

    @pl.when((y == 0) | (y == 3))
    def _():
        far = (y == 3).astype(jnp.int32)
        looped(CX, lambda x, k: column(x, k, 2 - 2 * far, 3, far), 4)

    @pl.when((y == 1) | (y == 2))
    def _():
        looped(CX, lambda x, k: column(x, k, 2 - y, 4, 0), 4)

    @pl.when(y == CY - 1)
    def _():
        for h in range(2):
            ghost_ref[:, h] = (
                total_ref[:, h * CH : (h + 1) * CH].astype(BF16).reshape(OWN_RUNS, RUN, CH)
            )


def back_kernel(
    grad_ref,
    env_ref,
    scale_ref,
    feat_ref,
    mix_ref,
    center_ref,
    radial_a_ref,
    radial_ref,
    couple_ref,
    down_ref,
    base_ref,
    slope_ref,
    normed_ref,
    pull_ref,
    direct_ref,
    grad_env_ref,
    grad_center_ref,
):
    y = pl.program_id(0)
    mask, atoms = atom_blocks()
    radial = radial_ref[...].astype(BF16)

    def column(x, k):
        i = x * CY + y
        harmonic = feature_rows(feat_ref, F_Y, 9, i)
        found = []
        for z in range(CZ):
            part = spans(z)
            grad = grad_ref[x, :, part]
            feature = jnp.concatenate(pair_features(harmonic, part, mask) + [atoms], 0)
            back = dims(feature, grad, 1, 1)
            table = jnp.concatenate(
                scaled_env(env_ref, couple_ref, i, z) + [radial, jnp.zeros((8, CH), BF16)], 0
            )
            found.append((back, dims(table, grad, 1, 0)))
        yield
        for z in range(CZ):
            part = spans(z)
            back, down = found[z]
            for m in range(9):
                grad_env_ref[m, rows_of(i, z), :] = back[m * PER_CELL : (m + 1) * PER_CELL]
            grad_center_ref[rows_of(i, z), :] = back[9 * PER_CELL :]
            rows = [down[9 * PER_CELL : 9 * PER_CELL + NBASIS]]
            for m in range(9):
                kept = jnp.where(mask, down[m * PER_CELL : (m + 1) * PER_CELL], 0.0)
                rows.append(jnp.sum(kept, 0, keepdims=True))
            down_ref[i, 0 : NBASIS + 9, part] = jnp.concatenate(rows, 0)

    looped(CX, column, 4)

    @pl.when(y == CY - 1)
    def _():
        invariants = [None] * 3
        for m in range(9):
            value = env_ref[m]
            squared = value * value
            degree = DEGREE[m]
            invariants[degree] = (
                squared if invariants[degree] is None else invariants[degree] + squared
            )
        normed, inverse = normalised(invariants)
        mixed = dims(jnp.concatenate(normed, 1).astype(BF16), mix_ref[...], 1, 0)
        gate = sigmoid_of(mixed)
        act = mixed * gate
        slope_ref[...] = gate + act - act * gate
        for d in range(3):
            normed_ref[d] = normed[d]
        high, low = halves(grad_center_ref[...])
        base_ref[...] = dims(high, center_ref[...], 1, 1) + dims(low, center_ref[...], 1, 1)
        scale = scale_ref[...]
        for m in range(9):
            pull_ref[m] = 2.0 * env_ref[m] * scale * inverse
        pulled = [
            grad_env_ref[m] * couple_ref[DEGREE[m] : DEGREE[m] + 1] * scale for m in range(9)
        ]
        direct_ref[...] = dims(
            jnp.concatenate(pulled, 1).astype(BF16),
            radial_blocks(radial_a_ref[...]).astype(BF16),
            1,
            1,
        )


def force_kernel(
    neigh_ref,
    base_ref,
    slope_ref,
    normed_ref,
    pull_env_ref,
    direct_ref,
    feat_ref,
    code_ref,
    down_ref,
    raw_ref,
    mix_ref,
    proj_ref,
    radial_ref,
    own_ref,
    ghost_ref,
    moment_ref,
    pull_ref,
):
    neigh = jnp.concatenate([neigh_ref[y, x] for x in range(CX) for y in range(CY)], 0)
    grad = base_ref[...] + dims(neigh.astype(BF16), proj_ref[...], 1, 1)
    grad = grad * slope_ref[...]
    grad = dims(grad.astype(BF16), mix_ref[...], 1, 1)
    grads = [grad[:, d * CH : (d + 1) * CH] for d in range(3)]
    normed = [normed_ref[d] for d in range(3)]
    mean = sum(jnp.sum(g * q, 1, keepdims=True) for g, q in zip(grads, normed)) * (1.0 / (3 * CH))
    grads = [g - q * mean for g, q in zip(grads, normed)]
    pulled = [pull_env_ref[m] * grads[DEGREE[m]] for m in range(9)]
    moment_ref[...] = direct_ref[...] + dims(
        jnp.concatenate(pulled, 1).astype(BF16),
        radial_blocks(radial_ref[...]).astype(BF16),
        1,
        1,
    )

    _, atoms = atom_blocks()
    row_slots = iota((PER_CELL, PAIRS), 0)
    ghost_ref[...] = jnp.zeros_like(ghost_ref)
    three, five, fifteen = math.sqrt(3.0), math.sqrt(5.0), math.sqrt(15.0)

    def column(i, k):
        harmonic = feature_rows(feat_ref, F_Y, 9, i)
        basis = feature_rows(feat_ref, F_B, NBASIS, i)
        slope = feature_rows(feat_ref, F_DB, NBASIS, i)
        weight = feature_rows(feat_ref, F_W, 1, i)
        weight_slope = feature_rows(feat_ref, F_DW, 1, i)
        inverse = feature_rows(feat_ref, F_INV, 1, i)
        parts = []
        for z in range(CZ):
            parts.append(dims(moment_ref[rows_of(i, z), :].astype(BF16), atoms, 0, 0))
        back = jnp.concatenate(parts, 1)
        yield
        weighted = basis * weight
        grad_weighted = jnp.zeros((NBASIS, PAIRS), F32)
        chain = []
        for m in range(9):
            block = back[m * NBASIS : (m + 1) * NBASIS]
            grad_weighted += block * harmonic[m : m + 1]
            if m:
                chain.append(
                    down_ref[i, NBASIS + m : NBASIS + m + 1, :]
                    + jnp.sum(block * weighted, 0, keepdims=True)
                )
        y1, y2, y3, y4, y5, y6, y7, y8 = chain
        grad_basis = down_ref[i, 0:NBASIS, :] + grad_weighted * weight
        grad_weight = raw_ref[pl.ds(i, 1), :] + jnp.sum(grad_weighted * basis, 0, keepdims=True)
        radial = jnp.sum(grad_basis * slope, 0, keepdims=True) + grad_weight * weight_slope
        nx, ny, nz = (harmonic[c : c + 1] * (1.0 / three) for c in range(1, 4))
        grad_x = three * y1 + fifteen * (ny * y4 + nz * y7 + nx * y8)
        grad_y = three * y2 + fifteen * (nx * y4 + nz * y5 - ny * y8)
        grad_z = three * y3 + fifteen * (ny * y5 + nx * y7) + (3.0 * five) * nz * y6
        along = radial - inverse * (nx * grad_x + ny * grad_y + nz * grad_z)
        pulls = (
            grad_x * inverse + nx * along,
            grad_y * inverse + ny * along,
            grad_z * inverse + nz * along,
        )
        yield
        x, y = i // CY, i % CY
        hot = hot_rows(5 * CELL_ROWS, code_ref[2, pl.ds(i, 1), :])
        mask = row_slots == code_ref[3, pl.ds(i, 1), :]
        for c in range(3):
            pull_ref[c, pl.ds(i, 1), :] = pulls[c]
        kept = jnp.concatenate([jnp.where(mask, pull, 0.0) for pull in pulls], 0)
        found = dims(hot, kept.astype(BF16), 1, 1)
        yield
        for dx in range(5):
            start = pl.multiple_of(((x + dx) * 8 + y) * 8, 8)
            ghost_ref[pl.ds(start, CELL_ROWS), :] += found[dx * CELL_ROWS : (dx + 1) * CELL_ROWS]

    looped(COLS, column, 8)

    gather = one_hot(iota((32, PAIRS), 0) == (iota((32, PAIRS), 1) >> 5))
    for c in range(3):
        high, low = halves(pull_ref[c])
        own_ref[c] = dims(high, gather, 1, 1) + dims(low, gather, 1, 1)


def call(kernel, outs, scratch, *args, by_y=(), by_y_out=(), micros=20):
    def spec(shape, moving):
        zeros = (0,) * len(shape)
        if not moving:
            return pl.BlockSpec(shape, lambda y: zeros)
        return pl.BlockSpec((shape[0] // CY,) + shape[1:], lambda y: (y,) + zeros[1:])

    grid = {}
    if by_y or by_y_out:
        grid = dict(
            grid=(CY,),
            in_specs=[spec(a.shape, k in by_y) for k, a in enumerate(args)],
            out_specs=[spec(shape, k in by_y_out) for k, (shape, _) in enumerate(outs)],
        )
    return pl.pallas_call(
        kernel,
        out_shape=[jax.ShapeDtypeStruct(shape, dtype) for shape, dtype in outs],
        scratch_shapes=[pltpu.VMEM(shape, dtype) for shape, dtype in scratch],
        compiler_params=pltpu.CompilerParams(vmem_limit_bytes=32 * 2**20),
        cost_estimate=pl.CostEstimate(
            flops=micros * 10**9, bytes_accessed=micros * 3 * 10**6, transcendentals=0
        ),
        **grid,
    )(*args)


def shifted(block, axis, distance):
    size = lax.axis_size(axis)
    return lax.ppermute(block, axis, [(i, (i + distance) % size) for i in range(size)])


def rims(array, axis, dim):
    length = array.shape[dim]
    before = shifted(lax.slice_in_dim(array, length - 2, length, axis=dim), axis, 1)
    after = shifted(lax.slice_in_dim(array, 0, 2, axis=dim), axis, -1)
    return before, after


def padded(array, axis, dim, tail=0, beside=None):
    before, after = rims(array, axis, dim)
    if beside is not None:
        before, beside = lax.optimization_barrier((before, beside))
    parts = [before, array, after]
    if tail:
        parts.append(jnp.zeros(after.shape[:dim] + (tail,) + after.shape[dim + 1 :], array.dtype))
    whole = jnp.concatenate(parts, axis=dim)
    return whole if beside is None else (whole, beside)


def folded(array, axis, dim, length):
    lower = lax.slice_in_dim(array, 0, 2, axis=dim).astype(BF16)
    upper = lax.slice_in_dim(array, length + 2, length + 4, axis=dim).astype(BF16)
    core = lax.slice_in_dim(array, 2, length + 2, axis=dim).astype(F32)
    to_first = shifted(upper, axis, 1).astype(F32)
    to_last = shifted(lower, axis, -1).astype(F32)
    if length == 2:
        return core + to_first + to_last
    return core + jnp.concatenate([to_first, to_last], axis=dim)


def shards(
    offsets,
    species,
    neighbours,
    counts,
    embed,
    radial_a,
    mix_in,
    proj_center,
    proj_neigh,
    radial_b,
    couple,
    latent_two,
    latent_three,
    readout,
):
    places = offsets.reshape(CX, CY, CZ, 48)
    numbers = neighbours.reshape(COLS, PAIRS)
    around, numbers = padded(places, "gx", 0, beside=numbers)
    rows = (counts.reshape(COLS, 32), species.reshape(1, ATOMS))
    around, rows = padded(around, "gy", 1, beside=rows)
    own = offsets.reshape(COLS, CZ, 3, PER_CELL).transpose(2, 0, 1, 3).reshape(3 * COLS, 32)
    around = padded(around, "gz", 2, tail=2)
    hidden, env, scale, feats, codes = call(
        env_kernel,
        [
            ((CY, CX, 32, CH), BF16),
            ((9, ATOMS, CH), F32),
            ((ATOMS, CH), F32),
            ((LANES * F_COUNT * COLS, 128), F32),
            ((4, COLS, PAIRS), jnp.int32),
        ],
        [((3, COLS, PAIRS), F32), ((ATOMS, 72), F32)],
        numbers,
        around.reshape(512, 48),
        own,
        *rows,
        embed,
        radial_a,
        mix_in,
    )
    grid = hidden.reshape(CY, CX, CZ, PER_CELL, CH)
    wide = padded(padded(grid, "gz", 2), "gx", 1)
    low, up = rims(wide, "gy", 0)
    (early,) = call(
        early_kernel,
        [((COLS, CH, PAIRS), F32)],
        [((OWN_RUNS * RUN, 2 * CH), BF16), ((ATOMS, CH), F32)],
        wide.reshape(OWN_RUNS, 2, RUN, CH),
        hidden,
        env,
        feats,
        codes,
        proj_center,
        proj_neigh,
        radial_b,
        couple,
        by_y_out=(0,),
    )
    energy, low_back, up_back, grads, raw = call(
        pair_kernel,
        [
            ((COLS, 32), F32),
            ((RIM_RUNS, 2, RUN, CH), BF16),
            ((RIM_RUNS, 2, RUN, CH), BF16),
            ((COLS, CH, PAIRS), BF16),
            ((COLS, PAIRS), F32),
        ],
        [
            ((2 * RIM_RUNS * RUN, 2 * CH), BF16),
            ((2 * RIM_RUNS * RUN, 2 * CH), F32),
            ((CX, 2 * SLAB, PAIRS), BF16),
        ],
        early,
        low.reshape(RIM_RUNS, 2, RUN, CH),
        up.reshape(RIM_RUNS, 2, RUN, CH),
        feats,
        codes,
        proj_neigh,
        latent_two,
        latent_three,
        readout.reshape(1, CH),
        by_y=(0,),
        by_y_out=(3,),
    )
    to_first = shifted(up_back, "gy", 1)
    to_last = shifted(low_back, "gy", -1)
    (ghost,) = call(
        spread_kernel,
        [((OWN_RUNS, 2, RUN, CH), BF16)],
        [((OWN_RUNS * RUN, 2 * CH), F32), ((CX, 4 * SLAB, PAIRS), BF16)],
        grads,
        codes,
        by_y=(0,),
    )
    ghost = ghost.astype(F32) + jnp.concatenate([to_first, to_last], 0).astype(F32)
    ghost = ghost.reshape(CY, CX + 4, CZ + 4, PER_CELL, CH)
    owned = folded(folded(ghost, "gx", 1, CX), "gz", 2, CZ)
    down, base, slope, normed, pull, direct = call(
        back_kernel,
        [
            ((COLS, 24, PAIRS), F32),
            ((ATOMS, CH), F32),
            ((ATOMS, CH), F32),
            ((3, ATOMS, CH), F32),
            ((9, ATOMS, CH), F32),
            ((ATOMS, 72), F32),
        ],
        [((9, ATOMS, CH), F32), ((ATOMS, CH), F32)],
        grads,
        env,
        scale,
        feats,
        mix_in,
        proj_center,
        radial_a,
        radial_b,
        couple,
        by_y=(0,),
    )
    own_pull, far_pull = call(
        force_kernel,
        [((3, COLS, 32), F32), ((512, 48), F32)],
        [((ATOMS, 72), F32), ((3, COLS, PAIRS), F32)],
        owned.reshape(CY, CX, 32, CH),
        base,
        slope,
        normed,
        pull,
        direct,
        feats,
        codes,
        down,
        raw,
        mix_in,
        proj_neigh,
        radial_a,
    )
    far = far_pull.reshape(CX + 4, CY + 4, 8, 48)
    far = folded(folded(folded(far, "gx", 0, CX), "gy", 1, CY), "gz", 2, CZ)
    near = own_pull.reshape(3, CX, CY, CZ, PER_CELL).transpose(1, 2, 3, 0, 4)
    forces = near - far.reshape(CX, CY, CZ, 3, PER_CELL)
    return (forces, energy.reshape(CX, CY, CZ, PER_CELL))


def solution(mesh):
    placed = (
        P("gx", "gy", "gz", None, None),
        P("gx", "gy", "gz", None),
        P("gx", "gy", "gz", None, None),
        P("gx", "gy", "gz", None),
    ) + (P(),) * 10
    return jax.shard_map(
        shards,
        mesh=mesh,
        in_specs=placed,
        out_specs=(P("gx", "gy", "gz", None, None), P("gx", "gy", "gz", None)),
        check_vma=False,
    )
```

profile of v0, /device:TPU:6, one launch (start us, length us, event | category | flops | bytes accessed | tf_op | source)
XLA Modules:
  0.0 148.2 jit_solution(10838082545981629077)
XLA Ops:
  0.7 0.8 fusion.11
  1.8 3.4 %collective-permute-start.1 = (f32[2,4,2,48]{3,2,1,0:T(2,128)S(1)}, f32[2,4,2,48]{3,2,1,0:T(2,128)S(1)}, u32[]{:S(2)}, u32[]{:S(2)}) collective-permute-start(f32[2,4,2,48]{3,2,1,0:T(2,128)S(1)} %slice.93), channel_id=1, source_target_pairs={{0,96},{32,0},{64,32},{96,64},{1,97},{33,1},{65,33},{97,65},{2,98}... | collective-permute-start | bytes 9224 | tf_op jit(solution)/shard_map/ppermute | solution.py:742
  5.1 0.8 copy.19
  6.0 1.1 reshape.63.nbr_ref
  7.2 0.5 collective-permute-start.2
  7.8 1.5 %collective-permute-start.3 = (f32[8,2,2,48]{3,2,1,0:T(2,128)S(1)}, f32[8,2,2,48]{3,2,1,0:T(2,128)S(1)}, u32[]{:S(2)}, u32[]{:S(2)}) collective-permute-start(f32[8,2,2,48]{3,2,1,0:T(2,128)S(1)} %get-tuple-element.73), channel_id=1, source_target_pairs={{0,24},{8,0},{16,8},{24,16},{1,25},{9,1},{17,9},{25,17},{2,26},{10... | collective-permute-start | bytes 18440 | tf_op jit(solution)/shard_map/ppermute | solution.py:742
  9.3 0.8 reshape.66.species_ref
  10.1 0.8 reshape.65.count_ref
  11.0 1.7 %collective-permute-done.3 = f32[8,2,2,48]{3,2,1,0:T(2,128)S(1)} collective-permute-done((f32[8,2,2,48]{3,2,1,0:T(2,128)S(1)}, f32[8,2,2,48]{3,2,1,0:T(2,128)S(1)}, u32[]{:S(2)}, u32[]{:S(2)}) %collective-permute-start.3) | collective-permute-done | bytes 6176 | tf_op jit(solution)/shard_map/ppermute | solution.py:742
  12.8 4.3 %collective-permute-start.5 = (f32[8,8,2,48]{3,2,1,0:T(2,128)S(1)}, f32[8,8,2,48]{3,2,1,0:T(2,128)S(1)}, u32[]{:S(2)}, u32[]{:S(2)}) collective-permute-start(f32[8,8,2,48]{3,2,1,0:T(2,128)S(1)} %pad_maximum_fusion.2), channel_id=1, source_target_pairs={{0,7},{1,0},{2,1},{3,2},{4,3},{5,4},{6,5},{7,6},{8,15},{9,8},{10,9... | collective-permute-start | bytes 73736 | tf_op jit(solution)/shard_map/ppermute | solution.py:742
  17.1 0.8 copy_bitcast_fusion
  18.1 1.5 collective-permute-done.5
  19.6 4.3 %collective-permute-done.4 = f32[8,8,2,48]{3,2,1,0:T(2,128)S(1)} collective-permute-done((f32[8,8,2,48]{3,2,1,0:T(2,128)S(1)}, f32[8,8,2,48]{3,2,1,0:T(2,128)S(1)}, u32[]{:S(2)}, u32[]{:S(2)}) %collective-permute-start.4) | collective-permute-done | bytes 24608 | tf_op jit(solution)/shard_map/ppermute | solution.py:742
  23.9 0.1 maximum_maximum_fusion
  24.0 6.8 %shard_map.149 = (bf16[4,4,32,128]{3,2,1,0:T(8,128)(2,1)S(1)}, f32[9,512,128]{2,1,0:T(8,128)S(1)}, f32[512,128]{1,0:T(8,128)S(1)}, f32[3584,128]{1,0:T(8,128)S(1)}, s32[4,16,1024]{2,1,0:T(8,128)S(1)}) custom-call(s32[16,1024]{1,0:T(8,128)S(1)} %reshape.63.nbr_ref, f32[512,48]{1,0:T(8,128)S(1)} %bitcast.26, f32[48,32]{1,0:T(8,128)S(1)} %reshape.69.own_ref, ...), custom_call_target="tpu_custom_call" | custom-call | flops 20000000000 | bytes 60000000 | tf_op jit(solution)/shard_map/pallas_call | solution.py:728
  30.9 0.4 collective-permute-start.7
  31.2 1.7 %collective-permute-start.6 = (bf16[4,4,2,16,128]{4,3,2,1,0:T(8,128)(2,1)S(1)}, bf16[4,4,2,16,128]{4,3,2,1,0:T(8,128)(2,1)S(1)}, u32[]{:S(2)}, u32[]{:S(2)}) collective-permute-start(bf16[4,4,2,16,128]{4,3,2,1,0:T(8,128)(2,1)S(1)} %bitcast.22), channel_id=1, source_target_pairs={{0,1},{1,2},{2,3},{3,4},{4,5},{5,6},{6,7},{7,0},{8,9},{9,10},{10,1... | collective-permute-start | bytes 393224 | tf_op jit(solution)/shard_map/ppermute | solution.py:742
  33.0 6.0 %collective-permute-done.7 = bf16[4,4,2,16,128]{4,3,2,1,0:T(8,128)(2,1)S(1)} collective-permute-done((bf16[4,4,2,16,128]{4,3,2,1,0:T(8,128)(2,1)S(1)}, bf16[4,4,2,16,128]{4,3,2,1,0:T(8,128)(2,1)S(1)}, u32[]{:S(2)}, u32[]{:S(2)}) %collective-permute-start.7) | collective-permute-done | bytes 131104 | tf_op jit(solution)/shard_map/ppermute | solution.py:742
  39.2 3.3 %collective-permute-start.9 = (bf16[4,2,6,16,128]{4,3,2,1,0:T(8,128)(2,1)S(1)}, bf16[4,2,6,16,128]{4,3,2,1,0:T(8,128)(2,1)S(1)}, u32[]{:S(2)}, u32[]{:S(2)}) collective-permute-start(bf16[4,2,6,16,128]{4,3,2,1,0:T(8,128)(2,1)S(1)} %get-tuple-element.63), channel_id=1, source_target_pairs={{0,96},{32,0},{64,32},{96,64},{1,97},{33,1},{65,33},{97,65},{2,98}... | collective-permute-start | bytes 589832 | tf_op jit(solution)/shard_map/ppermute | solution.py:742
  42.4 3.3 %collective-permute-done.8 = bf16[4,2,6,16,128]{4,3,2,1,0:T(8,128)(2,1)S(1)} collective-permute-done((bf16[4,2,6,16,128]{4,3,2,1,0:T(8,128)(2,1)S(1)}, bf16[4,2,6,16,128]{4,3,2,1,0:T(8,128)(2,1)S(1)}, u32[]{:S(2)}, u32[]{:S(2)}) %collective-permute-start.8) | collective-permute-done | bytes 196640 | tf_op jit(solution)/shard_map/ppermute | solution.py:742
  45.7 0.5 collective-permute-done.9
  46.2 0.1 pad_maximum_fusion
  46.3 0.1 fusion.6
  46.4 0.4 collective-permute-start.11
  46.9 3.1 %collective-permute-start.10 = (bf16[2,8,6,16,128]{4,3,2,1,0:T(8,128)(2,1)S(1)}, bf16[2,8,6,16,128]{4,3,2,1,0:T(8,128)(2,1)S(1)}, u32[]{:S(2)}, u32[]{:S(2)}) collective-permute-start(bf16[2,8,6,16,128]{4,3,2,1,0:T(8,128)(2,1)S(1)} %get-tuple-element.59), channel_id=1, source_target_pairs={{0,8},{8,16},{16,24},{24,0},{1,9},{9,17},{17,25},{25,1},{2,10},{10... | collective-permute-start | bytes 1179656 | tf_op jit(solution)/shard_map/ppermute | solution.py:742
  50.0 10.2 %shard_map.150.early_ref = f32[16,128,1024]{2,1,0:T(8,128)S(1)} custom-call(bf16[32,2,48,128]{3,2,1,0:T(8,128)(2,1)S(1)} %bitcast.20, bf16[4,4,32,128]{3,2,1,0:T(8,128)(2,1)S(1)} %get-tuple-element.30.hidden_ref, f32[9,512,128]{2,1,0:T(8,128)S(1)} %get-tuple-element.31.env_ref, f32[3584,128]{1,0:T(8,128)S(1)} %get-tuple-element.32.feat_ref, ...), custom_call_target="tpu_custom_call" | custom-call | flops 20000000000 | bytes 60000000 | tf_op jit(solution)/shard_map/pallas_call | solution.py:728
  60.3 19.5 %shard_map.151 = (f32[16,32]{1,0:T(8,128)S(1)}, bf16[16,2,48,128]{3,2,1,0:T(8,128)(2,1)S(1)}, bf16[16,2,48,128]{3,2,1,0:T(8,128)(2,1)S(1)}, bf16[16,128,1024]{2,1,0:T(8,128)(2,1)S(1)}, f32[16,1024]{1,0:T(8,128)S(1)}) custom-call(f32[16,128,1024]{2,1,0:T(8,128)S(1)} %shard_map.150.early_ref, bf16[16,2,48,128]{3,2,1,0:T(8,128)(2,1)S(1)} %bitcast.28, ...), custom_call_target="tpu_custom_call" | custom-call | flops 20000000000 | bytes 60000000 | tf_op jit(solution)/shard_map/pallas_call | solution.py:728
  79.8 2.1 %collective-permute-start.12 = (bf16[16,2,48,128]{3,2,1,0:T(8,128)(2,1)S(1)}, bf16[16,2,48,128]{3,2,1,0:T(8,128)(2,1)S(1)}, u32[]{:S(2)}, u32[]{:S(2)}) collective-permute-start(bf16[16,2,48,128]{3,2,1,0:T(8,128)(2,1)S(1)} %get-tuple-element.35), channel_id=1, source_target_pairs={{0,8},{8,16},{16,24},{24,0},{1,9},{9,17},{17,25},{25,1},{2,10},{10... | collective-permute-start | bytes 1179656 | tf_op jit(solution)/shard_map/ppermute | solution.py:742
  81.9 18.9 %shard_map.152 = bf16[32,2,48,128]{3,2,1,0:T(8,128)(2,1)S(1)} custom-call(bf16[16,128,1024]{2,1,0:T(8,128)(2,1)S(1)} %get-tuple-element.34.grad_ref, s32[4,16,1024]{2,1,0:T(8,128)S(1)} %get-tuple-element.33.code_ref), custom_call_target="tpu_custom_call" | custom-call | flops 20000000000 | bytes 60000000 | tf_op jit(solution)/shard_map/pallas_call | solution.py:728
  100.8 0.2 convert_add_fusion
  101.2 0.9 collective-permute-start.14
  102.2 2.4 %collective-permute-start.15 = (bf16[4,2,6,16,128]{4,3,2,1,0:T(8,128)(2,1)S(1)}, bf16[4,2,6,16,128]{4,3,2,1,0:T(8,128)(2,1)S(1)}, u32[]{:S(2)}, u32[]{:S(2)}) collective-permute-start(bf16[4,2,6,16,128]{4,3,2,1,0:T(8,128)(2,1)S(1)} %get-tuple-element.57), channel_id=1, source_target_pairs={{0,96},{32,0},{64,32},{96,64},{1,97},{33,1},{65,33},{97,65},{2,98}... | collective-permute-start | bytes 589832 | tf_op jit(solution)/shard_map/ppermute | solution.py:742
  104.5 3.3 %collective-permute-done.14 = bf16[4,2,6,16,128]{4,3,2,1,0:T(8,128)(2,1)S(1)} collective-permute-done((bf16[4,2,6,16,128]{4,3,2,1,0:T(8,128)(2,1)S(1)}, bf16[4,2,6,16,128]{4,3,2,1,0:T(8,128)(2,1)S(1)}, u32[]{:S(2)}, u32[]{:S(2)}) %collective-permute-start.14) | collective-permute-done | bytes 196640 | tf_op jit(solution)/shard_map/ppermute | solution.py:742
  107.9 1.1 collective-permute-done.15
  109.0 0.1 fusion.4
  109.3 4.1 %collective-permute-start.17 = (bf16[4,4,2,16,128]{4,3,2,1,0:T(8,128)(2,1)S(1)}, bf16[4,4,2,16,128]{4,3,2,1,0:T(8,128)(2,1)S(1)}, u32[]{:S(2)}, u32[]{:S(2)}) collective-permute-start(bf16[4,4,2,16,128]{4,3,2,1,0:T(8,128)(2,1)S(1)} %get-tuple-element.61), channel_id=1, source_target_pairs={{0,7},{1,0},{2,1},{3,2},{4,3},{5,4},{6,5},{7,6},{8,15},{9,8},{10,9... | collective-permute-start | bytes 393224 | tf_op jit(solution)/shard_map/ppermute | solution.py:742
  113.4 4.6 %shard_map.153 = (f32[16,24,1024]{2,1,0:T(8,128)S(1)}, f32[512,128]{1,0:T(8,128)S(1)}, f32[512,128]{1,0:T(8,128)S(1)}, f32[3,512,128]{2,1,0:T(8,128)S(1)}, f32[9...) custom-call(bf16[16,128,1024]{2,1,0:T(8,128)(2,1)S(1)} %get-tuple-element.34.grad_ref, ...), custom_call_target="tpu_custom_call" | custom-call | flops 20000000000 | bytes 60000000 | tf_op jit(solution)/shard_map/pallas_call | solution.py:728
  118.0 7.1 %shard_map.154 = (f32[3,16,32]{2,1,0:T(8,128)S(1)}, f32[512,48]{1,0:T(8,128)S(1)}) custom-call(f32[4,4,32,128]{3,2,1,0:T(8,128)S(1)} %bitcast.25, f32[512,128]{1,0:T(8,128)S(1)} %get-tuple-element.38.base_ref, f32[512,128]{1,0:T(8,128)S(1)} %get-tuple-element.39.slope_ref, f32[3,512,128]{2,1,0:T(8,128)S(1)} %get-tuple-element.40.normed_ref, ...), custom_call_target="tpu_custom_call" | custom-call | flops 20000000000 | bytes 60000000 | tf_op jit(solution)/shard_map/pallas_call | solution.py:728
  125.2 3.0 %collective-permute-start.19 = (bf16[2,8,8,48]{3,2,1,0:T(8,128)(2,1)S(1)}, bf16[2,8,8,48]{3,2,1,0:T(8,128)(2,1)S(1)}, u32[]{:S(2)}, u32[]{:S(2)}) collective-permute-start(bf16[2,8,8,48]{3,2,1,0:T(8,128)(2,1)S(1)} %bitcast.34), channel_id=1, source_target_pairs={{0,96},{32,0},{64,32},{96,64},{1,97},{33,1},{65,33},{97,65},{2,98}... | collective-permute-start | bytes 36872 | tf_op jit(solution)/shard_map/ppermute | solution.py:742
  128.2 1.6 %collective-permute-done.19 = bf16[2,8,8,48]{3,2,1,0:T(8,128)(2,1)S(1)} collective-permute-done((bf16[2,8,8,48]{3,2,1,0:T(8,128)(2,1)S(1)}, bf16[2,8,8,48]{3,2,1,0:T(8,128)(2,1)S(1)}, u32[]{:S(2)}, u32[]{:S(2)}) %collective-permute-start.19) | collective-permute-done | bytes 12320 | tf_op jit(solution)/shard_map/ppermute | solution.py:742
  129.8 3.2 %collective-permute-done.18 = bf16[2,8,8,48]{3,2,1,0:T(8,128)(2,1)S(1)} collective-permute-done((bf16[2,8,8,48]{3,2,1,0:T(8,128)(2,1)S(1)}, bf16[2,8,8,48]{3,2,1,0:T(8,128)(2,1)S(1)}, u32[]{:S(2)}, u32[]{:S(2)}) %collective-permute-start.18) | collective-permute-done | bytes 12320 | tf_op jit(solution)/shard_map/ppermute | solution.py:742
  133.1 3.2 %collective-permute-start.20 = (bf16[4,2,8,48]{3,2,1,0:T(8,128)(2,1)S(1)}, bf16[4,2,8,48]{3,2,1,0:T(8,128)(2,1)S(1)}, u32[]{:S(2)}, u32[]{:S(2)}) collective-permute-start(bf16[4,2,8,48]{3,2,1,0:T(8,128)(2,1)S(1)} %get-tuple-element.66), channel_id=1, source_target_pairs={{0,8},{8,16},{16,24},{24,0},{1,9},{9,17},{17,25},{25,1},{2,10},{10... | collective-permute-start | bytes 18440 | tf_op jit(solution)/shard_map/ppermute | solution.py:742
  136.3 1.4 collective-permute-done.20
  137.8 3.5 %collective-permute-done.21 = bf16[4,2,8,48]{3,2,1,0:T(8,128)(2,1)S(1)} collective-permute-done((bf16[4,2,8,48]{3,2,1,0:T(8,128)(2,1)S(1)}, bf16[4,2,8,48]{3,2,1,0:T(8,128)(2,1)S(1)}, u32[]{:S(2)}, u32[]{:S(2)}) %collective-permute-start.21) | collective-permute-done | bytes 6176 | tf_op jit(solution)/shard_map/ppermute | solution.py:742
  141.4 4.1 %collective-permute-start.23 = (bf16[4,4,2,48]{3,2,1,0:T(2,128)(2,1)S(1)}, bf16[4,4,2,48]{3,2,1,0:T(2,128)(2,1)S(1)}, u32[]{:S(2)}, u32[]{:S(2)}) collective-permute-start(bf16[4,4,2,48]{3,2,1,0:T(2,128)(2,1)S(1)} %get-tuple-element.71), channel_id=1, source_target_pairs={{0,7},{1,0},{2,1},{3,2},{4,3},{5,4},{6,5},{7,6},{8,15},{9,8},{10,9... | collective-permute-start | bytes 9224 | tf_op jit(solution)/shard_map/ppermute | solution.py:742
  145.5 0.7 reshape.79
  146.3 0.8 collective-permute-done.22
  147.3 0.6 copy.23
  (69 shorter events, 1.7 us)
Async XLA Ops:
  0.6 23.4 %copy-start = (bf16[384,128]{1,0:T(8,128)(2,1)S(1)}, bf16[384,128]{1,0:T(8,128)(2,1)}, u32[]{:S(2)}) copy-start(bf16[384,128]{1,0:T(8,128)(2,1)} %mix_ref.5) | copy-start | bytes 294916
  0.6 23.4 %copy-start.6 = (f32[8,128]{1,0:T(8,128)S(1)}, f32[8,128]{1,0:T(8,128)}, u32[]{:S(2)}) copy-start(f32[8,128]{1,0:T(8,128)} %radial_ref.7) | copy-start | bytes 12292
  0.7 23.4 %copy-start.7 = (f32[4,128]{1,0:T(4,128)S(1)}, f32[4,128]{1,0:T(4,128)}, u32[]{:S(2)}) copy-start(f32[4,128]{1,0:T(4,128)} %embed_ref.1) | copy-start | bytes 6148
  1.6 5.6 %collective-permute-start = (f32[2,4,2,48]{3,2,1,0:T(2,128)S(1)}, f32[2,4,2,48]{3,2,1,0:T(2,128)S(1)}, u32[]{:S(2)}, u32[]{:S(2)}) collective-permute-start(f32[2,4,2,48]{3,2,1,0:T(2,128)S(1)} %slice.91), channel_id=1, source_target_pairs={{0,32},{32,64},{64,96},{96,0},{1,33},{33,65},{65,97},{97,1},{2,34}... | collective-permute-start | bytes 9224 | tf_op jit(solution)/shard_map/ppermute | solution.py:742
  1.8 5.4 %collective-permute-start.1 = (f32[2,4,2,48]{3,2,1,0:T(2,128)S(1)}, f32[2,4,2,48]{3,2,1,0:T(2,128)S(1)}, u32[]{:S(2)}, u32[]{:S(2)}) collective-permute-start(f32[2,4,2,48]{3,2,1,0:T(2,128)S(1)} %slice.93), channel_id=1, source_target_pairs={{0,96},{32,0},{64,32},{96,64},{1,97},{33,1},{65,33},{97,65},{2,98}... | collective-permute-start | bytes 9224 | tf_op jit(solution)/shard_map/ppermute | solution.py:742
  7.2 3.8 %collective-permute-start.2 = (f32[8,2,2,48]{3,2,1,0:T(2,128)S(1)}, f32[8,2,2,48]{3,2,1,0:T(2,128)S(1)}, u32[]{:S(2)}, u32[]{:S(2)}) collective-permute-start(f32[8,2,2,48]{3,2,1,0:T(2,128)S(1)} %get-tuple-element.72), channel_id=1, source_target_pairs={{0,8},{8,16},{16,24},{24,0},{1,9},{9,17},{17,25},{25,1},{2,10},{10... | collective-permute-start | bytes 18440 | tf_op jit(solution)/shard_map/ppermute | solution.py:742
  7.8 4.9 %collective-permute-start.3 = (f32[8,2,2,48]{3,2,1,0:T(2,128)S(1)}, f32[8,2,2,48]{3,2,1,0:T(2,128)S(1)}, u32[]{:S(2)}, u32[]{:S(2)}) collective-permute-start(f32[8,2,2,48]{3,2,1,0:T(2,128)S(1)} %get-tuple-element.73), channel_id=1, source_target_pairs={{0,24},{8,0},{16,8},{24,16},{1,25},{9,1},{17,9},{25,17},{2,26},{10... | collective-permute-start | bytes 18440 | tf_op jit(solution)/shard_map/ppermute | solution.py:742
  12.8 6.8 %collective-permute-start.5 = (f32[8,8,2,48]{3,2,1,0:T(2,128)S(1)}, f32[8,8,2,48]{3,2,1,0:T(2,128)S(1)}, u32[]{:S(2)}, u32[]{:S(2)}) collective-permute-start(f32[8,8,2,48]{3,2,1,0:T(2,128)S(1)} %pad_maximum_fusion.2), channel_id=1, source_target_pairs={{0,7},{1,0},{2,1},{3,2},{4,3},{5,4},{6,5},{7,6},{8,15},{9,8},{10,9... | collective-permute-start | bytes 73736 | tf_op jit(solution)/shard_map/ppermute | solution.py:742
  17.1 6.7 %collective-permute-start.4 = (f32[8,8,2,48]{3,2,1,0:T(2,128)S(1)}, f32[8,8,2,48]{3,2,1,0:T(2,128)S(1)}, u32[]{:S(2)}, u32[]{:S(2)}) collective-permute-start(f32[8,8,2,48]{3,2,1,0:T(2,128)S(1)} %pad_maximum_fusion.2), channel_id=1, source_target_pairs={{0,1},{1,2},{2,3},{3,4},{4,5},{5,6},{6,7},{7,0},{8,9},{9,10},{10,1... | collective-permute-start | bytes 73736 | tf_op jit(solution)/shard_map/ppermute | solution.py:742
  30.9 8.1 %collective-permute-start.7 = (bf16[4,4,2,16,128]{4,3,2,1,0:T(8,128)(2,1)S(1)}, bf16[4,4,2,16,128]{4,3,2,1,0:T(8,128)(2,1)S(1)}, u32[]{:S(2)}, u32[]{:S(2)}) collective-permute-start(bf16[4,4,2,16,128]{4,3,2,1,0:T(8,128)(2,1)S(1)} %bitcast.21), channel_id=1, source_target_pairs={{0,7},{1,0},{2,1},{3,2},{4,3},{5,4},{6,5},{7,6},{8,15},{9,8},{10,9... | collective-permute-start | bytes 393224 | tf_op jit(solution)/shard_map/ppermute | solution.py:742
  31.2 7.7 %collective-permute-start.6 = (bf16[4,4,2,16,128]{4,3,2,1,0:T(8,128)(2,1)S(1)}, bf16[4,4,2,16,128]{4,3,2,1,0:T(8,128)(2,1)S(1)}, u32[]{:S(2)}, u32[]{:S(2)}) collective-permute-start(bf16[4,4,2,16,128]{4,3,2,1,0:T(8,128)(2,1)S(1)} %bitcast.22), channel_id=1, source_target_pairs={{0,1},{1,2},{2,3},{3,4},{4,5},{5,6},{6,7},{7,0},{8,9},{9,10},{10,1... | collective-permute-start | bytes 393224 | tf_op jit(solution)/shard_map/ppermute | solution.py:742
  39.0 6.7 %collective-permute-start.8 = (bf16[4,2,6,16,128]{4,3,2,1,0:T(8,128)(2,1)S(1)}, bf16[4,2,6,16,128]{4,3,2,1,0:T(8,128)(2,1)S(1)}, u32[]{:S(2)}, u32[]{:S(2)}) collective-permute-start(bf16[4,2,6,16,128]{4,3,2,1,0:T(8,128)(2,1)S(1)} %get-tuple-element.62), channel_id=1, source_target_pairs={{0,32},{32,64},{64,96},{96,0},{1,33},{33,65},{65,97},{97,1},{2,34}... | collective-permute-start | bytes 589832 | tf_op jit(solution)/shard_map/ppermute | solution.py:742
  39.1 10.9 %copy-start.3 = (bf16[128,128]{1,0:T(8,128)(2,1)S(1)}, bf16[128,128]{1,0:T(8,128)(2,1)}, u32[]{:S(2)}) copy-start(bf16[128,128]{1,0:T(8,128)(2,1)} %center_ref.3) | copy-start | bytes 98308
  39.1 10.9 %copy-start.4 = (bf16[128,128]{1,0:T(8,128)(2,1)S(1)}, bf16[128,128]{1,0:T(8,128)(2,1)}, u32[]{:S(2)}) copy-start(bf16[128,128]{1,0:T(8,128)(2,1)} %proj_ref.1) | copy-start | bytes 98308
  39.1 10.9 %copy-start.5 = (f32[8,128]{1,0:T(8,128)S(1)}, f32[8,128]{1,0:T(8,128)}, u32[]{:S(2)}) copy-start(f32[8,128]{1,0:T(8,128)} %radial_ref.6) | copy-start | bytes 12292
  39.1 10.9 %copy-start.8 = (f32[3,128]{1,0:T(4,128)S(1)}, f32[3,128]{1,0:T(4,128)}, u32[]{:S(2)}) copy-start(f32[3,128]{1,0:T(4,128)} %couple_ref.3) | copy-start | bytes 4612
  39.2 7.0 %collective-permute-start.9 = (bf16[4,2,6,16,128]{4,3,2,1,0:T(8,128)(2,1)S(1)}, bf16[4,2,6,16,128]{4,3,2,1,0:T(8,128)(2,1)S(1)}, u32[]{:S(2)}, u32[]{:S(2)}) collective-permute-start(bf16[4,2,6,16,128]{4,3,2,1,0:T(8,128)(2,1)S(1)} %get-tuple-element.63), channel_id=1, source_target_pairs={{0,96},{32,0},{64,32},{96,64},{1,97},{33,1},{65,33},{97,65},{2,98}... | collective-permute-start | bytes 589832 | tf_op jit(solution)/shard_map/ppermute | solution.py:742
  46.4 13.8 %collective-permute-start.11 = (bf16[2,8,6,16,128]{4,3,2,1,0:T(8,128)(2,1)S(1)}, bf16[2,8,6,16,128]{4,3,2,1,0:T(8,128)(2,1)S(1)}, u32[]{:S(2)}, u32[]{:S(2)}) collective-permute-start(bf16[2,8,6,16,128]{4,3,2,1,0:T(8,128)(2,1)S(1)} %get-tuple-element.58), channel_id=1, source_target_pairs={{0,24},{8,0},{16,8},{24,16},{1,25},{9,1},{17,9},{25,17},{2,26},{10... | collective-permute-start | bytes 1179656 | tf_op jit(solution)/shard_map/ppermute | solution.py:742
  46.9 13.4 %collective-permute-start.10 = (bf16[2,8,6,16,128]{4,3,2,1,0:T(8,128)(2,1)S(1)}, bf16[2,8,6,16,128]{4,3,2,1,0:T(8,128)(2,1)S(1)}, u32[]{:S(2)}, u32[]{:S(2)}) collective-permute-start(bf16[2,8,6,16,128]{4,3,2,1,0:T(8,128)(2,1)S(1)} %get-tuple-element.59), channel_id=1, source_target_pairs={{0,8},{8,16},{16,24},{24,0},{1,9},{9,17},{17,25},{25,1},{2,10},{10... | collective-permute-start | bytes 1179656 | tf_op jit(solution)/shard_map/ppermute | solution.py:742
  50.0 10.3 %copy-start.1 = (bf16[128,128]{1,0:T(8,128)(2,1)S(1)}, bf16[128,128]{1,0:T(8,128)(2,1)}, u32[]{:S(2)}) copy-start(bf16[128,128]{1,0:T(8,128)(2,1)} %two_ref.1) | copy-start | bytes 98308
  50.0 10.3 %copy-start.2 = (bf16[128,128]{1,0:T(8,128)(2,1)S(1)}, bf16[128,128]{1,0:T(8,128)(2,1)}, u32[]{:S(2)}) copy-start(bf16[128,128]{1,0:T(8,128)(2,1)} %three_ref.1) | copy-start | bytes 98308
  50.0 10.3 %copy-start.9 = (f32[128]{0:T(128)S(1)}, f32[128]{0:T(128)}, u32[]{:S(2)}) copy-start(f32[128]{0:T(128)} %param.27) | copy-start | bytes 1540
  79.8 21.0 %collective-permute-start.12 = (bf16[16,2,48,128]{3,2,1,0:T(8,128)(2,1)S(1)}, bf16[16,2,48,128]{3,2,1,0:T(8,128)(2,1)S(1)}, u32[]{:S(2)}, u32[]{:S(2)}) collective-permute-start(bf16[16,2,48,128]{3,2,1,0:T(8,128)(2,1)S(1)} %get-tuple-element.35), channel_id=1, source_target_pairs={{0,8},{8,16},{16,24},{24,0},{1,9},{9,17},{17,25},{25,1},{2,10},{10... | collective-permute-start | bytes 1179656 | tf_op jit(solution)/shard_map/ppermute | solution.py:742
  81.9 18.9 %collective-permute-start.13 = (bf16[16,2,48,128]{3,2,1,0:T(8,128)(2,1)S(1)}, bf16[16,2,48,128]{3,2,1,0:T(8,128)(2,1)S(1)}, u32[]{:S(2)}, u32[]{:S(2)}) collective-permute-start(bf16[16,2,48,128]{3,2,1,0:T(8,128)(2,1)S(1)} %get-tuple-element.36), channel_id=1, source_target_pairs={{0,24},{8,0},{16,8},{24,16},{1,25},{9,1},{17,9},{25,17},{2,26},{10... | collective-permute-start | bytes 1179656 | tf_op jit(solution)/shard_map/ppermute | solution.py:742
  101.2 6.7 %collective-permute-start.14 = (bf16[4,2,6,16,128]{4,3,2,1,0:T(8,128)(2,1)S(1)}, bf16[4,2,6,16,128]{4,3,2,1,0:T(8,128)(2,1)S(1)}, u32[]{:S(2)}, u32[]{:S(2)}) collective-permute-start(bf16[4,2,6,16,128]{4,3,2,1,0:T(8,128)(2,1)S(1)} %get-tuple-element.56), channel_id=1, source_target_pairs={{0,32},{32,64},{64,96},{96,0},{1,33},{33,65},{65,97},{97,1},{2,34}... | collective-permute-start | bytes 589832 | tf_op jit(solution)/shard_map/ppermute | solution.py:742
  102.2 6.8 %collective-permute-start.15 = (bf16[4,2,6,16,128]{4,3,2,1,0:T(8,128)(2,1)S(1)}, bf16[4,2,6,16,128]{4,3,2,1,0:T(8,128)(2,1)S(1)}, u32[]{:S(2)}, u32[]{:S(2)}) collective-permute-start(bf16[4,2,6,16,128]{4,3,2,1,0:T(8,128)(2,1)S(1)} %get-tuple-element.57), channel_id=1, source_target_pairs={{0,96},{32,0},{64,32},{96,64},{1,97},{33,1},{65,33},{97,65},{2,98}... | collective-permute-start | bytes 589832 | tf_op jit(solution)/shard_map/ppermute | solution.py:742
  109.2 8.8 %collective-permute-start.16 = (bf16[4,4,2,16,128]{4,3,2,1,0:T(8,128)(2,1)S(1)}, bf16[4,4,2,16,128]{4,3,2,1,0:T(8,128)(2,1)S(1)}, u32[]{:S(2)}, u32[]{:S(2)}) collective-permute-start(bf16[4,4,2,16,128]{4,3,2,1,0:T(8,128)(2,1)S(1)} %get-tuple-element.60), channel_id=1, source_target_pairs={{0,1},{1,2},{2,3},{3,4},{4,5},{5,6},{6,7},{7,0},{8,9},{9,10},{10,1... | collective-permute-start | bytes 393224 | tf_op jit(solution)/shard_map/ppermute | solution.py:742
  109.3 8.7 %collective-permute-start.17 = (bf16[4,4,2,16,128]{4,3,2,1,0:T(8,128)(2,1)S(1)}, bf16[4,4,2,16,128]{4,3,2,1,0:T(8,128)(2,1)S(1)}, u32[]{:S(2)}, u32[]{:S(2)}) collective-permute-start(bf16[4,4,2,16,128]{4,3,2,1,0:T(8,128)(2,1)S(1)} %get-tuple-element.61), channel_id=1, source_target_pairs={{0,7},{1,0},{2,1},{3,2},{4,3},{5,4},{6,5},{7,6},{8,15},{9,8},{10,9... | collective-permute-start | bytes 393224 | tf_op jit(solution)/shard_map/ppermute | solution.py:742
  125.2 4.6 %collective-permute-start.19 = (bf16[2,8,8,48]{3,2,1,0:T(8,128)(2,1)S(1)}, bf16[2,8,8,48]{3,2,1,0:T(8,128)(2,1)S(1)}, u32[]{:S(2)}, u32[]{:S(2)}) collective-permute-start(bf16[2,8,8,48]{3,2,1,0:T(8,128)(2,1)S(1)} %bitcast.34), channel_id=1, source_target_pairs={{0,96},{32,0},{64,32},{96,64},{1,97},{33,1},{65,33},{97,65},{2,98}... | collective-permute-start | bytes 36872 | tf_op jit(solution)/shard_map/ppermute | solution.py:742
  128.2 4.8 %collective-permute-start.18 = (bf16[2,8,8,48]{3,2,1,0:T(8,128)(2,1)S(1)}, bf16[2,8,8,48]{3,2,1,0:T(8,128)(2,1)S(1)}, u32[]{:S(2)}, u32[]{:S(2)}) collective-permute-start(bf16[2,8,8,48]{3,2,1,0:T(8,128)(2,1)S(1)} %bitcast.33), channel_id=1, source_target_pairs={{0,32},{32,64},{64,96},{96,0},{1,33},{33,65},{65,97},{97,1},{2,34}... | collective-permute-start | bytes 36872 | tf_op jit(solution)/shard_map/ppermute | solution.py:742
  133.1 4.7 %collective-permute-start.20 = (bf16[4,2,8,48]{3,2,1,0:T(8,128)(2,1)S(1)}, bf16[4,2,8,48]{3,2,1,0:T(8,128)(2,1)S(1)}, u32[]{:S(2)}, u32[]{:S(2)}) collective-permute-start(bf16[4,2,8,48]{3,2,1,0:T(8,128)(2,1)S(1)} %get-tuple-element.66), channel_id=1, source_target_pairs={{0,8},{8,16},{16,24},{24,0},{1,9},{9,17},{17,25},{25,1},{2,10},{10... | collective-permute-start | bytes 18440 | tf_op jit(solution)/shard_map/ppermute | solution.py:742
  136.3 4.9 %collective-permute-start.21 = (bf16[4,2,8,48]{3,2,1,0:T(8,128)(2,1)S(1)}, bf16[4,2,8,48]{3,2,1,0:T(8,128)(2,1)S(1)}, u32[]{:S(2)}, u32[]{:S(2)}) collective-permute-start(bf16[4,2,8,48]{3,2,1,0:T(8,128)(2,1)S(1)} %get-tuple-element.67), channel_id=1, source_target_pairs={{0,24},{8,0},{16,8},{24,16},{1,25},{9,1},{17,9},{25,17},{2,26},{10... | collective-permute-start | bytes 18440 | tf_op jit(solution)/shard_map/ppermute | solution.py:742
  141.3 5.8 %collective-permute-start.22 = (bf16[4,4,2,48]{3,2,1,0:T(2,128)(2,1)S(1)}, bf16[4,4,2,48]{3,2,1,0:T(2,128)(2,1)S(1)}, u32[]{:S(2)}, u32[]{:S(2)}) collective-permute-start(bf16[4,4,2,48]{3,2,1,0:T(2,128)(2,1)S(1)} %get-tuple-element.70), channel_id=1, source_target_pairs={{0,1},{1,2},{2,3},{3,4},{4,5},{5,6},{6,7},{7,0},{8,9},{9,10},{10,1... | collective-permute-start | bytes 9224 | tf_op jit(solution)/shard_map/ppermute | solution.py:742
  141.4 5.8 %collective-permute-start.23 = (bf16[4,4,2,48]{3,2,1,0:T(2,128)(2,1)S(1)}, bf16[4,4,2,48]{3,2,1,0:T(2,128)(2,1)S(1)}, u32[]{:S(2)}, u32[]{:S(2)}) collective-permute-start(bf16[4,4,2,48]{3,2,1,0:T(2,128)(2,1)S(1)} %get-tuple-element.71), channel_id=1, source_target_pairs={{0,7},{1,0},{2,1},{3,2},{4,3},{5,4},{6,5},{7,6},{8,15},{9,8},{10,9... | collective-permute-start | bytes 9224 | tf_op jit(solution)/shard_map/ppermute | solution.py:742
where the time goes:
time: 151 us; the launch traced here: 148 us
  Pallas kernels  67.1 us (44%)
  starting transfers between devices  38.9 us (26%)
  waiting for transfers between devices  32.4 us (21%)
  local copies, waits for them, and re-layouts  7.49 us (5%)
    pallas_call x6, Pallas kernels, call(): pl.pallas_call(kernel, out_shape=[jax.ShapeDtypeStruct(shape, dtype) for...  67.1 us
    ppermute x24, starting transfers between devices, shifted(): lax.ppermute(block, axis, [(i, (i + distance) % size) for i in range(size)])  38.9 us
    ppermute x24, waiting for transfers between devices, shifted(): lax.ppermute(block, axis, [(i, (i + distance) % size) for i in range(size)])  32.4 us
  transfers between devices with their start and end apart: 24, of which 14 were waited for; matrix products, arithmetic and copies ran while one was open for 4% of the time, Pallas kernels for 23%

commit v1 on v0

--- a/solution.py
+++ b/solution.py
@@ -101,10 +101,11 @@
 
 
 def gated(half):
+    half = half.astype(BF16)
     t = jnp.tanh(half)
-    up = t + 1.0
+    up = t + 1
     act = half * up
-    return act, up + act * (1.0 - t)
+    return act, up + act * (1 - t)
 
 
 def sigmoid_of(v):
@@ -446,20 +447,19 @@
         yield
         value = early_ref[x] + jnp.where(upper, fetched[CH:], fetched[:CH])
         one, slope_one = gated(value)
-        value = dims(two_half, one.astype(BF16), 0, 0)
+        value = dims(two_half, one, 0, 0)
         yield
         two, slope_two = gated(value)
-        value = dims(three_half, two.astype(BF16), 0, 0)
+        value = dims(three_half, two, 0, 0)
         yield
         top, slope_top = gated(value)
-        raw_ref[pl.ds(i, 1), :] = 2.0 * jnp.sum(top * readout, 0, keepdims=True)
-        grad = slope_top * (readout * weight)
-        grad = dims(three_half, grad.astype(BF16), 1, 0)
-        yield
-        grad = dims(two_half, (grad * slope_two).astype(BF16), 1, 0)
-        yield
-        grad = grad * slope_one
-        grad = grad.astype(BF16)
+        raw_ref[pl.ds(i, 1), :] = 2.0 * jnp.sum(top.astype(F32) * readout, 0, keepdims=True)
+        grad = slope_top * (readout * weight).astype(BF16)
+        grad = dims(three_half, grad, 1, 0)
+        yield
+        grad = dims(two_half, grad.astype(BF16) * slope_two, 1, 0)
+        yield
+        grad = grad.astype(BF16) * slope_one
         high = grad * jnp.where(upper, 1.0, 0.0).astype(BF16)
         spread = jnp.concatenate([grad - high, high], 0)
         grad_ref[x] = grad
@@ -627,10 +627,11 @@
     mix_ref,
     proj_ref,
     radial_ref,
-    own_ref,
+    low_out_ref,
+    core_ref,
+    up_out_ref,
+    moment_ref,
     ghost_ref,
-    moment_ref,
-    pull_ref,
 ):
     neigh = jnp.concatenate([neigh_ref[y, x] for x in range(CX) for y in range(CY)], 0)
     grad = base_ref[...] + dims(neigh.astype(BF16), proj_ref[...], 1, 1)
@@ -650,6 +651,8 @@
 
     _, atoms = atom_blocks()
     row_slots = iota((PER_CELL, PAIRS), 0)
+    own_slots = row_slots == ((iota((PER_CELL, PAIRS), 1) & (CELL_PAIRS - 1)) >> 5)
+    own_cells = one_hot(iota((8, PAIRS), 0) == 2 + (iota((8, PAIRS), 1) >> 9))
     ghost_ref[...] = jnp.zeros_like(ghost_ref)
     three, five, fifteen = math.sqrt(3.0), math.sqrt(5.0), math.sqrt(15.0)
 
@@ -694,21 +697,22 @@
         x, y = i // CY, i % CY
         hot = hot_rows(5 * CELL_ROWS, code_ref[2, pl.ds(i, 1), :])
         mask = row_slots == code_ref[3, pl.ds(i, 1), :]
-        for c in range(3):
-            pull_ref[c, pl.ds(i, 1), :] = pulls[c]
+        owned = jnp.concatenate([jnp.where(own_slots, pull, 0.0) for pull in pulls], 0)
+        own_found = dims(own_cells, owned.astype(BF16), 1, 1)
         kept = jnp.concatenate([jnp.where(mask, pull, 0.0) for pull in pulls], 0)
         found = dims(hot, kept.astype(BF16), 1, 1)
         yield
         for dx in range(5):
             start = pl.multiple_of(((x + dx) * 8 + y) * 8, 8)
-            ghost_ref[pl.ds(start, CELL_ROWS), :] += found[dx * CELL_ROWS : (dx + 1) * CELL_ROWS]
+            ghost_ref[pl.ds(start, CELL_ROWS), :] -= found[dx * CELL_ROWS : (dx + 1) * CELL_ROWS]
+        start = pl.multiple_of(((x + 2) * 8 + y + 2) * 8, 8)
+        ghost_ref[pl.ds(start, 8), :] += own_found
 
     looped(COLS, column, 8)
 
-    gather = one_hot(iota((32, PAIRS), 0) == (iota((32, PAIRS), 1) >> 5))
-    for c in range(3):
-        high, low = halves(pull_ref[c])
-        own_ref[c] = dims(high, gather, 1, 1) + dims(low, gather, 1, 1)
+    low_out_ref[...] = ghost_ref[:128].astype(BF16)
+    core_ref[...] = ghost_ref[128:384]
+    up_out_ref[...] = ghost_ref[384:].astype(BF16)
 
 
 def call(kernel, outs, scratch, *args, by_y=(), by_y_out=(), micros=20):
@@ -891,10 +895,10 @@
         couple,
         by_y=(0,),
     )
-    own_pull, far_pull = call(
+    low, core, up = call(
         force_kernel,
-        [((3, COLS, 32), F32), ((512, 48), F32)],
-        [((ATOMS, 72), F32), ((3, COLS, PAIRS), F32)],
+        [((128, 48), BF16), ((256, 48), F32), ((128, 48), BF16)],
+        [((ATOMS, 72), F32), ((512, 48), F32)],
         owned.reshape(CY, CX, 32, CH),
         base,
         slope,
@@ -909,10 +913,12 @@
         proj_neigh,
         radial_a,
     )
-    far = far_pull.reshape(CX + 4, CY + 4, 8, 48)
-    far = folded(folded(folded(far, "gx", 0, CX), "gy", 1, CY), "gz", 2, CZ)
-    near = own_pull.reshape(3, CX, CY, CZ, PER_CELL).transpose(1, 2, 3, 0, 4)
-    forces = near - far.reshape(CX, CY, CZ, 3, PER_CELL)
+    to_first = shifted(up, "gx", 1)
+    to_last = shifted(low, "gx", -1)
+    pulls = core + jnp.concatenate([to_first, to_last], 0).astype(F32)
+    pulls = pulls.reshape(CX, CY + 4, 8, 48)
+    pulls = folded(folded(pulls, "gy", 1, CY), "gz", 2, CZ)
+    forces = pulls.reshape(CX, CY, CZ, 3, PER_CELL)
     return (forces, energy.reshape(CX, CY, CZ, PER_CELL))
 
 

time: 151 us -> 135 us (0.89)
  Pallas kernels: 67.1 us -> 55.4 us
  waiting for transfers between devices: 32.4 us -> 30.5 us
    pallas_call x6, Pallas kernels: 67.1 us -> 55.4 us  [call(): pl.pallas_call(kernel, out_shape=[jax.ShapeDtypeStruct(shape, dtype) for...]
    ppermute x24, waiting for transfers between devices: 32.4 us -> 30.5 us  [shifted(): lax.ppermute(block, axis, [(i, (i + distance) % size) for i in range(size)])]
  transfers between devices with their start and end apart: 24 -> 24, of which waited for: 14 -> 15; matrix products, arithmetic and copies ran while one was open for 4% -> 4% of each run, Pallas kernels for 23% -> 18%
where the time goes in v1:
time: 135 us; the launch traced here: 133 us
  Pallas kernels  55.4 us (41%)
  starting transfers between devices  38.1 us (28%)
  waiting for transfers between devices  30.5 us (23%)
  local copies, waits for them, and re-layouts  7.38 us (5%)
    pallas_call x6, Pallas kernels, call(): pl.pallas_call(kernel, out_shape=[jax.ShapeDtypeStruct(shape, dtype) for...  55.4 us
    ppermute x24, starting transfers between devices, shifted(): lax.ppermute(block, axis, [(i, (i + distance) % size) for i in range(size)])  38.1 us
    ppermute x24, waiting for transfers between devices, shifted(): lax.ppermute(block, axis, [(i, (i + distance) % size) for i in range(size)])  30.5 us
  transfers between devices with their start and end apart: 24, of which 15 were waited for; matrix products, arithmetic and copies ran while one was open for 4% of the time, Pallas kernels for 18%

profile of v1, /device:TPU:6, one launch (start us, length us, event | category | flops | bytes accessed | tf_op | source)
XLA Modules:
  0.0 133.3 jit_solution(13367329759350064419)
XLA Ops:
  0.7 0.8 fusion.9
  1.8 3.4 %collective-permute-start.1 = (f32[2,4,2,48]{3,2,1,0:T(2,128)S(1)}, f32[2,4,2,48]{3,2,1,0:T(2,128)S(1)}, u32[]{:S(2)}, u32[]{:S(2)}) collective-permute-start(f32[2,4,2,48]{3,2,1,0:T(2,128)S(1)} %slice.77), channel_id=1, source_target_pairs={{0,96},{32,0},{64,32},{96,64},{1,97},{33,1},{65,33},{97,65},{2,98}... | collective-permute-start | bytes 9224 | tf_op jit(solution)/shard_map/ppermute | solution.py:746
  5.1 0.8 copy.31
  6.0 1.1 reshape.57.nbr_ref
  7.2 0.5 collective-permute-start.2
  7.8 1.5 %collective-permute-start.3 = (f32[8,2,2,48]{3,2,1,0:T(2,128)S(1)}, f32[8,2,2,48]{3,2,1,0:T(2,128)S(1)}, u32[]{:S(2)}, u32[]{:S(2)}) collective-permute-start(f32[8,2,2,48]{3,2,1,0:T(2,128)S(1)} %get-tuple-element.75), channel_id=1, source_target_pairs={{0,24},{8,0},{16,8},{24,16},{1,25},{9,1},{17,9},{25,17},{2,26},{10... | collective-permute-start | bytes 18440 | tf_op jit(solution)/shard_map/ppermute | solution.py:746
  9.3 0.8 reshape.60.species_ref
  10.1 0.8 reshape.59.count_ref
  11.0 1.7 %collective-permute-done.3 = f32[8,2,2,48]{3,2,1,0:T(2,128)S(1)} collective-permute-done((f32[8,2,2,48]{3,2,1,0:T(2,128)S(1)}, f32[8,2,2,48]{3,2,1,0:T(2,128)S(1)}, u32[]{:S(2)}, u32[]{:S(2)}) %collective-permute-start.3) | collective-permute-done | bytes 6176 | tf_op jit(solution)/shard_map/ppermute | solution.py:746
  12.8 4.3 %collective-permute-start.5 = (f32[8,8,2,48]{3,2,1,0:T(2,128)S(1)}, f32[8,8,2,48]{3,2,1,0:T(2,128)S(1)}, u32[]{:S(2)}, u32[]{:S(2)}) collective-permute-start(f32[8,8,2,48]{3,2,1,0:T(2,128)S(1)} %pad_maximum_fusion.2), channel_id=1, source_target_pairs={{0,7},{1,0},{2,1},{3,2},{4,3},{5,4},{6,5},{7,6},{8,15},{9,8},{10,9... | collective-permute-start | bytes 73736 | tf_op jit(solution)/shard_map/ppermute | solution.py:746
  17.1 0.8 copy_bitcast_fusion
  18.1 1.5 %collective-permute-done.5 = f32[8,8,2,48]{3,2,1,0:T(2,128)S(1)} collective-permute-done((f32[8,8,2,48]{3,2,1,0:T(2,128)S(1)}, f32[8,8,2,48]{3,2,1,0:T(2,128)S(1)}, u32[]{:S(2)}, u32[]{:S(2)}) %collective-permute-start.5) | collective-permute-done | bytes 24608 | tf_op jit(solution)/shard_map/ppermute | solution.py:746
  19.6 4.3 %collective-permute-done.4 = f32[8,8,2,48]{3,2,1,0:T(2,128)S(1)} collective-permute-done((f32[8,8,2,48]{3,2,1,0:T(2,128)S(1)}, f32[8,8,2,48]{3,2,1,0:T(2,128)S(1)}, u32[]{:S(2)}, u32[]{:S(2)}) %collective-permute-start.4) | collective-permute-done | bytes 24608 | tf_op jit(solution)/shard_map/ppermute | solution.py:746
  24.0 6.8 %shard_map.149 = (bf16[4,4,32,128]{3,2,1,0:T(8,128)(2,1)S(1)}, f32[9,512,128]{2,1,0:T(8,128)S(1)}, f32[512,128]{1,0:T(8,128)S(1)}, f32[3584,128]{1,0:T(8,128)S(1)}, s32[4,16,1024]{2,1,0:T(8,128)S(1)}) custom-call(s32[16,1024]{1,0:T(8,128)S(1)} %reshape.57.nbr_ref, f32[512,48]{1,0:T(8,128)S(1)} %bitcast.22, f32[48,32]{1,0:T(8,128)S(1)} %reshape.63.own_ref, ...), custom_call_target="tpu_custom_call" | custom-call | flops 20000000000 | bytes 60000000 | tf_op jit(solution)/shard_map/pallas_call | solution.py:732
  30.9 0.4 collective-permute-start.7
  31.2 1.7 %collective-permute-start.6 = (bf16[4,4,2,16,128]{4,3,2,1,0:T(8,128)(2,1)S(1)}, bf16[4,4,2,16,128]{4,3,2,1,0:T(8,128)(2,1)S(1)}, u32[]{:S(2)}, u32[]{:S(2)}) collective-permute-start(bf16[4,4,2,16,128]{4,3,2,1,0:T(8,128)(2,1)S(1)} %bitcast.18), channel_id=1, source_target_pairs={{0,1},{1,2},{2,3},{3,4},{4,5},{5,6},{6,7},{7,0},{8,9},{9,10},{10,1... | collective-permute-start | bytes 393224 | tf_op jit(solution)/shard_map/ppermute | solution.py:746
  33.0 6.0 %collective-permute-done.7 = bf16[4,4,2,16,128]{4,3,2,1,0:T(8,128)(2,1)S(1)} collective-permute-done((bf16[4,4,2,16,128]{4,3,2,1,0:T(8,128)(2,1)S(1)}, bf16[4,4,2,16,128]{4,3,2,1,0:T(8,128)(2,1)S(1)}, u32[]{:S(2)}, u32[]{:S(2)}) %collective-permute-start.7) | collective-permute-done | bytes 131104 | tf_op jit(solution)/shard_map/ppermute | solution.py:746
  39.1 3.3 %collective-permute-start.9 = (bf16[4,2,6,16,128]{4,3,2,1,0:T(8,128)(2,1)S(1)}, bf16[4,2,6,16,128]{4,3,2,1,0:T(8,128)(2,1)S(1)}, u32[]{:S(2)}, u32[]{:S(2)}) collective-permute-start(bf16[4,2,6,16,128]{4,3,2,1,0:T(8,128)(2,1)S(1)} %get-tuple-element.67), channel_id=1, source_target_pairs={{0,96},{32,0},{64,32},{96,64},{1,97},{33,1},{65,33},{97,65},{2,98}... | collective-permute-start | bytes 589832 | tf_op jit(solution)/shard_map/ppermute | solution.py:746
  42.4 3.3 %collective-permute-done.8 = bf16[4,2,6,16,128]{4,3,2,1,0:T(8,128)(2,1)S(1)} collective-permute-done((bf16[4,2,6,16,128]{4,3,2,1,0:T(8,128)(2,1)S(1)}, bf16[4,2,6,16,128]{4,3,2,1,0:T(8,128)(2,1)S(1)}, u32[]{:S(2)}, u32[]{:S(2)}) %collective-permute-start.8) | collective-permute-done | bytes 196640 | tf_op jit(solution)/shard_map/ppermute | solution.py:746
  45.7 0.5 collective-permute-done.9
  46.3 0.1 fusion.5
  46.4 0.4 collective-permute-start.11
  46.8 2.9 %collective-permute-start.10 = (bf16[2,8,6,16,128]{4,3,2,1,0:T(8,128)(2,1)S(1)}, bf16[2,8,6,16,128]{4,3,2,1,0:T(8,128)(2,1)S(1)}, u32[]{:S(2)}, u32[]{:S(2)}) collective-permute-start(bf16[2,8,6,16,128]{4,3,2,1,0:T(8,128)(2,1)S(1)} %get-tuple-element.63), channel_id=1, source_target_pairs={{0,8},{8,16},{16,24},{24,0},{1,9},{9,17},{17,25},{25,1},{2,10},{10... | collective-permute-start | bytes 1179656 | tf_op jit(solution)/shard_map/ppermute | solution.py:746
  49.8 10.2 %shard_map.150.early_ref = f32[16,128,1024]{2,1,0:T(8,128)S(1)} custom-call(bf16[32,2,48,128]{3,2,1,0:T(8,128)(2,1)S(1)} %bitcast.16, bf16[4,4,32,128]{3,2,1,0:T(8,128)(2,1)S(1)} %get-tuple-element.31.hidden_ref, f32[9,512,128]{2,1,0:T(8,128)S(1)} %get-tuple-element.32.env_ref, f32[3584,128]{1,0:T(8,128)S(1)} %get-tuple-element.33.feat_ref, ...), custom_call_target="tpu_custom_call" | custom-call | flops 20000000000 | bytes 60000000 | tf_op jit(solution)/shard_map/pallas_call | solution.py:732
  60.1 17.4 %shard_map.151 = (f32[16,32]{1,0:T(8,128)S(1)}, bf16[16,2,48,128]{3,2,1,0:T(8,128)(2,1)S(1)}, bf16[16,2,48,128]{3,2,1,0:T(8,128)(2,1)S(1)}, bf16[16,128,1024]{2,1,0:T(8,128)(2,1)S(1)}, f32[16,1024]{1,0:T(8,128)S(1)}) custom-call(f32[16,128,1024]{2,1,0:T(8,128)S(1)} %shard_map.150.early_ref, bf16[16,2,48,128]{3,2,1,0:T(8,128)(2,1)S(1)} %bitcast.24, ...), custom_call_target="tpu_custom_call" | custom-call | flops 20000000000 | bytes 60000000 | tf_op jit(solution)/shard_map/pallas_call | solution.py:732
  77.5 2.3 %collective-permute-start.12 = (bf16[16,2,48,128]{3,2,1,0:T(8,128)(2,1)S(1)}, bf16[16,2,48,128]{3,2,1,0:T(8,128)(2,1)S(1)}, u32[]{:S(2)}, u32[]{:S(2)}) collective-permute-start(bf16[16,2,48,128]{3,2,1,0:T(8,128)(2,1)S(1)} %get-tuple-element.36), channel_id=1, source_target_pairs={{0,8},{8,16},{16,24},{24,0},{1,9},{9,17},{17,25},{25,1},{2,10},{10... | collective-permute-start | bytes 1179656 | tf_op jit(solution)/shard_map/ppermute | solution.py:746
  79.8 9.1 %shard_map.152 = bf16[32,2,48,128]{3,2,1,0:T(8,128)(2,1)S(1)} custom-call(bf16[16,128,1024]{2,1,0:T(8,128)(2,1)S(1)} %get-tuple-element.35.grad_ref, s32[4,16,1024]{2,1,0:T(8,128)S(1)} %get-tuple-element.34.code_ref), custom_call_target="tpu_custom_call" | custom-call | flops 20000000000 | bytes 60000000 | tf_op jit(solution)/shard_map/pallas_call | solution.py:732
  88.9 0.3 collective-permute-done.12
  89.2 3.2 %collective-permute-done.13 = bf16[16,2,48,128]{3,2,1,0:T(8,128)(2,1)S(1)} collective-permute-done((bf16[16,2,48,128]{3,2,1,0:T(8,128)(2,1)S(1)}, bf16[16,2,48,128]{3,2,1,0:T(8,128)(2,1)S(1)}, u32[]{:S(2)}, u32[]{:S(2)}) %collective-permute-start.13) | collective-permute-done | bytes 393248 | tf_op jit(solution)/shard_map/ppermute | solution.py:746
  92.4 0.2 convert_add_fusion
  92.8 3.2 %collective-permute-start.15 = (bf16[4,2,6,16,128]{4,3,2,1,0:T(8,128)(2,1)S(1)}, bf16[4,2,6,16,128]{4,3,2,1,0:T(8,128)(2,1)S(1)}, u32[]{:S(2)}, u32[]{:S(2)}) collective-permute-start(bf16[4,2,6,16,128]{4,3,2,1,0:T(8,128)(2,1)S(1)} %get-tuple-element.61), channel_id=1, source_target_pairs={{0,96},{32,0},{64,32},{96,64},{1,97},{33,1},{65,33},{97,65},{2,98}... | collective-permute-start | bytes 589832 | tf_op jit(solution)/shard_map/ppermute | solution.py:746
  96.1 3.3 %collective-permute-done.14 = bf16[4,2,6,16,128]{4,3,2,1,0:T(8,128)(2,1)S(1)} collective-permute-done((bf16[4,2,6,16,128]{4,3,2,1,0:T(8,128)(2,1)S(1)}, bf16[4,2,6,16,128]{4,3,2,1,0:T(8,128)(2,1)S(1)}, u32[]{:S(2)}, u32[]{:S(2)}) %collective-permute-start.14) | collective-permute-done | bytes 196640 | tf_op jit(solution)/shard_map/ppermute | solution.py:746
  99.4 0.6 collective-permute-done.15
  100.1 0.1 fusion.3
  100.3 4.1 %collective-permute-start.17 = (bf16[4,4,2,16,128]{4,3,2,1,0:T(8,128)(2,1)S(1)}, bf16[4,4,2,16,128]{4,3,2,1,0:T(8,128)(2,1)S(1)}, u32[]{:S(2)}, u32[]{:S(2)}) collective-permute-start(bf16[4,4,2,16,128]{4,3,2,1,0:T(8,128)(2,1)S(1)} %get-tuple-element.65), channel_id=1, source_target_pairs={{0,7},{1,0},{2,1},{3,2},{4,3},{5,4},{6,5},{7,6},{8,15},{9,8},{10,9... | collective-permute-start | bytes 393224 | tf_op jit(solution)/shard_map/ppermute | solution.py:746
  104.4 4.6 %shard_map.153 = (f32[16,24,1024]{2,1,0:T(8,128)S(1)}, f32[512,128]{1,0:T(8,128)S(1)}, f32[512,128]{1,0:T(8,128)S(1)}, f32[3,512,128]{2,1,0:T(8,128)S(1)}, f32[9...) custom-call(bf16[16,128,1024]{2,1,0:T(8,128)(2,1)S(1)} %get-tuple-element.35.grad_ref, ...), custom_call_target="tpu_custom_call" | custom-call | flops 20000000000 | bytes 60000000 | tf_op jit(solution)/shard_map/pallas_call | solution.py:732
  109.1 7.3 %shard_map.154 = (bf16[128,48]{1,0:T(8,128)(2,1)S(1)}, f32[256,48]{1,0:T(8,128)S(1)}, bf16[128,48]{1,0:T(8,128)(2,1)S(1)}) custom-call(f32[4,4,32,128]{3,2,1,0:T(8,128)S(1)} %bitcast.21, f32[512,128]{1,0:T(8,128)S(1)} %get-tuple-element.39.base_ref, f32[512,128]{1,0:T(8,128)S(1)} %get-tuple-element.40.slope_ref, ...), custom_call_target="tpu_custom_call" | custom-call | flops 20000000000 | bytes 60000000 | tf_op jit(solution)/shard_map/pallas_call | solution.py:732
  116.4 1.5 %collective-permute-start.18 = (bf16[128,48]{1,0:T(8,128)(2,1)S(1)}, bf16[128,48]{1,0:T(8,128)(2,1)S(1)}, u32[]{:S(2)}, u32[]{:S(2)}) collective-permute-start(bf16[128,48]{1,0:T(8,128)(2,1)S(1)} %get-tuple-element.47), channel_id=1, source_target_pairs={{0,32},{32,64},{64,96},{96,0},{1,33},{33,65},{65,97},{97,1},{2,34}... | collective-permute-start | bytes 36872 | tf_op jit(solution)/shard_map/ppermute | solution.py:746
  117.9 1.8 %collective-permute-start.19 = (bf16[128,48]{1,0:T(8,128)(2,1)S(1)}, bf16[128,48]{1,0:T(8,128)(2,1)S(1)}, u32[]{:S(2)}, u32[]{:S(2)}) collective-permute-start(bf16[128,48]{1,0:T(8,128)(2,1)S(1)} %get-tuple-element.48), channel_id=1, source_target_pairs={{0,96},{32,0},{64,32},{96,64},{1,97},{33,1},{65,33},{97,65},{2,98}... | collective-permute-start | bytes 36872 | tf_op jit(solution)/shard_map/ppermute | solution.py:746
  119.7 1.6 %collective-permute-done.18 = bf16[128,48]{1,0:T(8,128)(2,1)S(1)} collective-permute-done((bf16[128,48]{1,0:T(8,128)(2,1)S(1)}, bf16[128,48]{1,0:T(8,128)(2,1)S(1)}, u32[]{:S(2)}, u32[]{:S(2)}) %collective-permute-start.18) | collective-permute-done | bytes 12320 | tf_op jit(solution)/shard_map/ppermute | solution.py:746
  121.3 0.4 collective-permute-start.20
  121.7 1.7 %collective-permute-start.21 = (bf16[4,2,8,48]{3,2,1,0:T(8,128)(2,1)S(1)}, bf16[4,2,8,48]{3,2,1,0:T(8,128)(2,1)S(1)}, u32[]{:S(2)}, u32[]{:S(2)}) collective-permute-start(bf16[4,2,8,48]{3,2,1,0:T(8,128)(2,1)S(1)} %get-tuple-element.69), channel_id=1, source_target_pairs={{0,24},{8,0},{16,8},{24,16},{1,25},{9,1},{17,9},{25,17},{2,26},{10... | collective-permute-start | bytes 18440 | tf_op jit(solution)/shard_map/ppermute | solution.py:746
  123.4 1.7 %collective-permute-done.20 = bf16[4,2,8,48]{3,2,1,0:T(8,128)(2,1)S(1)} collective-permute-done((bf16[4,2,8,48]{3,2,1,0:T(8,128)(2,1)S(1)}, bf16[4,2,8,48]{3,2,1,0:T(8,128)(2,1)S(1)}, u32[]{:S(2)}, u32[]{:S(2)}) %collective-permute-start.20) | collective-permute-done | bytes 6176 | tf_op jit(solution)/shard_map/ppermute | solution.py:746
  125.1 1.5 %collective-permute-done.21 = bf16[4,2,8,48]{3,2,1,0:T(8,128)(2,1)S(1)} collective-permute-done((bf16[4,2,8,48]{3,2,1,0:T(8,128)(2,1)S(1)}, bf16[4,2,8,48]{3,2,1,0:T(8,128)(2,1)S(1)}, u32[]{:S(2)}, u32[]{:S(2)}) %collective-permute-start.21) | collective-permute-done | bytes 6176 | tf_op jit(solution)/shard_map/ppermute | solution.py:746
  126.8 4.1 %collective-permute-start.23 = (bf16[4,4,2,48]{3,2,1,0:T(2,128)(2,1)S(1)}, bf16[4,4,2,48]{3,2,1,0:T(2,128)(2,1)S(1)}, u32[]{:S(2)}, u32[]{:S(2)}) collective-permute-start(bf16[4,4,2,48]{3,2,1,0:T(2,128)(2,1)S(1)} %get-tuple-element.73), channel_id=1, source_target_pairs={{0,7},{1,0},{2,1},{3,2},{4,3},{5,4},{6,5},{7,6},{8,15},{9,8},{10,9... | collective-permute-start | bytes 9224 | tf_op jit(solution)/shard_map/ppermute | solution.py:746
  130.9 0.7 reshape.73
  131.6 0.9 collective-permute-done.22
  132.7 0.6 copy.34
  (65 shorter events, 1.8 us)
Async XLA Ops:
  0.6 23.4 %copy-start = (bf16[384,128]{1,0:T(8,128)(2,1)S(1)}, bf16[384,128]{1,0:T(8,128)(2,1)}, u32[]{:S(2)}) copy-start(bf16[384,128]{1,0:T(8,128)(2,1)} %mix_ref.5) | copy-start | bytes 294916
  0.6 23.4 %copy-start.6 = (f32[8,128]{1,0:T(8,128)S(1)}, f32[8,128]{1,0:T(8,128)}, u32[]{:S(2)}) copy-start(f32[8,128]{1,0:T(8,128)} %radial_ref.7) | copy-start | bytes 12292
  0.7 23.4 %copy-start.7 = (f32[4,128]{1,0:T(4,128)S(1)}, f32[4,128]{1,0:T(4,128)}, u32[]{:S(2)}) copy-start(f32[4,128]{1,0:T(4,128)} %embed_ref.1) | copy-start | bytes 6148
  1.6 5.6 %collective-permute-start = (f32[2,4,2,48]{3,2,1,0:T(2,128)S(1)}, f32[2,4,2,48]{3,2,1,0:T(2,128)S(1)}, u32[]{:S(2)}, u32[]{:S(2)}) collective-permute-start(f32[2,4,2,48]{3,2,1,0:T(2,128)S(1)} %slice.75), channel_id=1, source_target_pairs={{0,32},{32,64},{64,96},{96,0},{1,33},{33,65},{65,97},{97,1},{2,34}... | collective-permute-start | bytes 9224 | tf_op jit(solution)/shard_map/ppermute | solution.py:746
  1.8 5.4 %collective-permute-start.1 = (f32[2,4,2,48]{3,2,1,0:T(2,128)S(1)}, f32[2,4,2,48]{3,2,1,0:T(2,128)S(1)}, u32[]{:S(2)}, u32[]{:S(2)}) collective-permute-start(f32[2,4,2,48]{3,2,1,0:T(2,128)S(1)} %slice.77), channel_id=1, source_target_pairs={{0,96},{32,0},{64,32},{96,64},{1,97},{33,1},{65,33},{97,65},{2,98}... | collective-permute-start | bytes 9224 | tf_op jit(solution)/shard_map/ppermute | solution.py:746
  7.2 3.8 %collective-permute-start.2 = (f32[8,2,2,48]{3,2,1,0:T(2,128)S(1)}, f32[8,2,2,48]{3,2,1,0:T(2,128)S(1)}, u32[]{:S(2)}, u32[]{:S(2)}) collective-permute-start(f32[8,2,2,48]{3,2,1,0:T(2,128)S(1)} %get-tuple-element.74), channel_id=1, source_target_pairs={{0,8},{8,16},{16,24},{24,0},{1,9},{9,17},{17,25},{25,1},{2,10},{10... | collective-permute-start | bytes 18440 | tf_op jit(solution)/shard_map/ppermute | solution.py:746
  7.8 4.9 %collective-permute-start.3 = (f32[8,2,2,48]{3,2,1,0:T(2,128)S(1)}, f32[8,2,2,48]{3,2,1,0:T(2,128)S(1)}, u32[]{:S(2)}, u32[]{:S(2)}) collective-permute-start(f32[8,2,2,48]{3,2,1,0:T(2,128)S(1)} %get-tuple-element.75), channel_id=1, source_target_pairs={{0,24},{8,0},{16,8},{24,16},{1,25},{9,1},{17,9},{25,17},{2,26},{10... | collective-permute-start | bytes 18440 | tf_op jit(solution)/shard_map/ppermute | solution.py:746
  12.8 6.8 %collective-permute-start.5 = (f32[8,8,2,48]{3,2,1,0:T(2,128)S(1)}, f32[8,8,2,48]{3,2,1,0:T(2,128)S(1)}, u32[]{:S(2)}, u32[]{:S(2)}) collective-permute-start(f32[8,8,2,48]{3,2,1,0:T(2,128)S(1)} %pad_maximum_fusion.2), channel_id=1, source_target_pairs={{0,7},{1,0},{2,1},{3,2},{4,3},{5,4},{6,5},{7,6},{8,15},{9,8},{10,9... | collective-permute-start | bytes 73736 | tf_op jit(solution)/shard_map/ppermute | solution.py:746
  17.1 6.7 %collective-permute-start.4 = (f32[8,8,2,48]{3,2,1,0:T(2,128)S(1)}, f32[8,8,2,48]{3,2,1,0:T(2,128)S(1)}, u32[]{:S(2)}, u32[]{:S(2)}) collective-permute-start(f32[8,8,2,48]{3,2,1,0:T(2,128)S(1)} %pad_maximum_fusion.2), channel_id=1, source_target_pairs={{0,1},{1,2},{2,3},{3,4},{4,5},{5,6},{6,7},{7,0},{8,9},{9,10},{10,1... | collective-permute-start | bytes 73736 | tf_op jit(solution)/shard_map/ppermute | solution.py:746
  30.9 8.1 %collective-permute-start.7 = (bf16[4,4,2,16,128]{4,3,2,1,0:T(8,128)(2,1)S(1)}, bf16[4,4,2,16,128]{4,3,2,1,0:T(8,128)(2,1)S(1)}, u32[]{:S(2)}, u32[]{:S(2)}) collective-permute-start(bf16[4,4,2,16,128]{4,3,2,1,0:T(8,128)(2,1)S(1)} %bitcast.17), channel_id=1, source_target_pairs={{0,7},{1,0},{2,1},{3,2},{4,3},{5,4},{6,5},{7,6},{8,15},{9,8},{10,9... | collective-permute-start | bytes 393224 | tf_op jit(solution)/shard_map/ppermute | solution.py:746
  31.2 7.7 %collective-permute-start.6 = (bf16[4,4,2,16,128]{4,3,2,1,0:T(8,128)(2,1)S(1)}, bf16[4,4,2,16,128]{4,3,2,1,0:T(8,128)(2,1)S(1)}, u32[]{:S(2)}, u32[]{:S(2)}) collective-permute-start(bf16[4,4,2,16,128]{4,3,2,1,0:T(8,128)(2,1)S(1)} %bitcast.18), channel_id=1, source_target_pairs={{0,1},{1,2},{2,3},{3,4},{4,5},{5,6},{6,7},{7,0},{8,9},{9,10},{10,1... | collective-permute-start | bytes 393224 | tf_op jit(solution)/shard_map/ppermute | solution.py:746
  39.0 6.7 %collective-permute-start.8 = (bf16[4,2,6,16,128]{4,3,2,1,0:T(8,128)(2,1)S(1)}, bf16[4,2,6,16,128]{4,3,2,1,0:T(8,128)(2,1)S(1)}, u32[]{:S(2)}, u32[]{:S(2)}) collective-permute-start(bf16[4,2,6,16,128]{4,3,2,1,0:T(8,128)(2,1)S(1)} %get-tuple-element.66), channel_id=1, source_target_pairs={{0,32},{32,64},{64,96},{96,0},{1,33},{33,65},{65,97},{97,1},{2,34}... | collective-permute-start | bytes 589832 | tf_op jit(solution)/shard_map/ppermute | solution.py:746
  39.1 10.7 %copy-start.3 = (bf16[128,128]{1,0:T(8,128)(2,1)S(1)}, bf16[128,128]{1,0:T(8,128)(2,1)}, u32[]{:S(2)}) copy-start(bf16[128,128]{1,0:T(8,128)(2,1)} %center_ref.3) | copy-start | bytes 98308
  39.1 10.6 %copy-start.4 = (bf16[128,128]{1,0:T(8,128)(2,1)S(1)}, bf16[128,128]{1,0:T(8,128)(2,1)}, u32[]{:S(2)}) copy-start(bf16[128,128]{1,0:T(8,128)(2,1)} %proj_ref.1) | copy-start | bytes 98308
  39.1 10.6 %copy-start.5 = (f32[8,128]{1,0:T(8,128)S(1)}, f32[8,128]{1,0:T(8,128)}, u32[]{:S(2)}) copy-start(f32[8,128]{1,0:T(8,128)} %radial_ref.6) | copy-start | bytes 12292
  39.1 10.6 %copy-start.8 = (f32[3,128]{1,0:T(4,128)S(1)}, f32[3,128]{1,0:T(4,128)}, u32[]{:S(2)}) copy-start(f32[3,128]{1,0:T(4,128)} %couple_ref.3) | copy-start | bytes 4612
  39.1 7.0 %collective-permute-start.9 = (bf16[4,2,6,16,128]{4,3,2,1,0:T(8,128)(2,1)S(1)}, bf16[4,2,6,16,128]{4,3,2,1,0:T(8,128)(2,1)S(1)}, u32[]{:S(2)}, u32[]{:S(2)}) collective-permute-start(bf16[4,2,6,16,128]{4,3,2,1,0:T(8,128)(2,1)S(1)} %get-tuple-element.67), channel_id=1, source_target_pairs={{0,96},{32,0},{64,32},{96,64},{1,97},{33,1},{65,33},{97,65},{2,98}... | collective-permute-start | bytes 589832 | tf_op jit(solution)/shard_map/ppermute | solution.py:746
  46.4 13.6 %collective-permute-start.11 = (bf16[2,8,6,16,128]{4,3,2,1,0:T(8,128)(2,1)S(1)}, bf16[2,8,6,16,128]{4,3,2,1,0:T(8,128)(2,1)S(1)}, u32[]{:S(2)}, u32[]{:S(2)}) collective-permute-start(bf16[2,8,6,16,128]{4,3,2,1,0:T(8,128)(2,1)S(1)} %get-tuple-element.62), channel_id=1, source_target_pairs={{0,24},{8,0},{16,8},{24,16},{1,25},{9,1},{17,9},{25,17},{2,26},{10... | collective-permute-start | bytes 1179656 | tf_op jit(solution)/shard_map/ppermute | solution.py:746
  46.8 13.2 %collective-permute-start.10 = (bf16[2,8,6,16,128]{4,3,2,1,0:T(8,128)(2,1)S(1)}, bf16[2,8,6,16,128]{4,3,2,1,0:T(8,128)(2,1)S(1)}, u32[]{:S(2)}, u32[]{:S(2)}) collective-permute-start(bf16[2,8,6,16,128]{4,3,2,1,0:T(8,128)(2,1)S(1)} %get-tuple-element.63), channel_id=1, source_target_pairs={{0,8},{8,16},{16,24},{24,0},{1,9},{9,17},{17,25},{25,1},{2,10},{10... | collective-permute-start | bytes 1179656 | tf_op jit(solution)/shard_map/ppermute | solution.py:746
  49.8 10.3 %copy-start.1 = (bf16[128,128]{1,0:T(8,128)(2,1)S(1)}, bf16[128,128]{1,0:T(8,128)(2,1)}, u32[]{:S(2)}) copy-start(bf16[128,128]{1,0:T(8,128)(2,1)} %two_ref.1) | copy-start | bytes 98308
  49.8 10.3 %copy-start.2 = (bf16[128,128]{1,0:T(8,128)(2,1)S(1)}, bf16[128,128]{1,0:T(8,128)(2,1)}, u32[]{:S(2)}) copy-start(bf16[128,128]{1,0:T(8,128)(2,1)} %three_ref.1) | copy-start | bytes 98308
  49.8 10.3 %copy-start.9 = (f32[128]{0:T(128)S(1)}, f32[128]{0:T(128)}, u32[]{:S(2)}) copy-start(f32[128]{0:T(128)} %param.27) | copy-start | bytes 1540
  77.5 11.7 %collective-permute-start.12 = (bf16[16,2,48,128]{3,2,1,0:T(8,128)(2,1)S(1)}, bf16[16,2,48,128]{3,2,1,0:T(8,128)(2,1)S(1)}, u32[]{:S(2)}, u32[]{:S(2)}) collective-permute-start(bf16[16,2,48,128]{3,2,1,0:T(8,128)(2,1)S(1)} %get-tuple-element.36), channel_id=1, source_target_pairs={{0,8},{8,16},{16,24},{24,0},{1,9},{9,17},{17,25},{25,1},{2,10},{10... | collective-permute-start | bytes 1179656 | tf_op jit(solution)/shard_map/ppermute | solution.py:746
  79.8 12.6 %collective-permute-start.13 = (bf16[16,2,48,128]{3,2,1,0:T(8,128)(2,1)S(1)}, bf16[16,2,48,128]{3,2,1,0:T(8,128)(2,1)S(1)}, u32[]{:S(2)}, u32[]{:S(2)}) collective-permute-start(bf16[16,2,48,128]{3,2,1,0:T(8,128)(2,1)S(1)} %get-tuple-element.37), channel_id=1, source_target_pairs={{0,24},{8,0},{16,8},{24,16},{1,25},{9,1},{17,9},{25,17},{2,26},{10... | collective-permute-start | bytes 1179656 | tf_op jit(solution)/shard_map/ppermute | solution.py:746
  92.7 6.7 %collective-permute-start.14 = (bf16[4,2,6,16,128]{4,3,2,1,0:T(8,128)(2,1)S(1)}, bf16[4,2,6,16,128]{4,3,2,1,0:T(8,128)(2,1)S(1)}, u32[]{:S(2)}, u32[]{:S(2)}) collective-permute-start(bf16[4,2,6,16,128]{4,3,2,1,0:T(8,128)(2,1)S(1)} %get-tuple-element.60), channel_id=1, source_target_pairs={{0,32},{32,64},{64,96},{96,0},{1,33},{33,65},{65,97},{97,1},{2,34}... | collective-permute-start | bytes 589832 | tf_op jit(solution)/shard_map/ppermute | solution.py:746
  92.8 7.2 %collective-permute-start.15 = (bf16[4,2,6,16,128]{4,3,2,1,0:T(8,128)(2,1)S(1)}, bf16[4,2,6,16,128]{4,3,2,1,0:T(8,128)(2,1)S(1)}, u32[]{:S(2)}, u32[]{:S(2)}) collective-permute-start(bf16[4,2,6,16,128]{4,3,2,1,0:T(8,128)(2,1)S(1)} %get-tuple-element.61), channel_id=1, source_target_pairs={{0,96},{32,0},{64,32},{96,64},{1,97},{33,1},{65,33},{97,65},{2,98}... | collective-permute-start | bytes 589832 | tf_op jit(solution)/shard_map/ppermute | solution.py:746
  100.2 8.8 %collective-permute-start.16 = (bf16[4,4,2,16,128]{4,3,2,1,0:T(8,128)(2,1)S(1)}, bf16[4,4,2,16,128]{4,3,2,1,0:T(8,128)(2,1)S(1)}, u32[]{:S(2)}, u32[]{:S(2)}) collective-permute-start(bf16[4,4,2,16,128]{4,3,2,1,0:T(8,128)(2,1)S(1)} %get-tuple-element.64), channel_id=1, source_target_pairs={{0,1},{1,2},{2,3},{3,4},{4,5},{5,6},{6,7},{7,0},{8,9},{9,10},{10,1... | collective-permute-start | bytes 393224 | tf_op jit(solution)/shard_map/ppermute | solution.py:746
  100.3 8.7 %collective-permute-start.17 = (bf16[4,4,2,16,128]{4,3,2,1,0:T(8,128)(2,1)S(1)}, bf16[4,4,2,16,128]{4,3,2,1,0:T(8,128)(2,1)S(1)}, u32[]{:S(2)}, u32[]{:S(2)}) collective-permute-start(bf16[4,4,2,16,128]{4,3,2,1,0:T(8,128)(2,1)S(1)} %get-tuple-element.65), channel_id=1, source_target_pairs={{0,7},{1,0},{2,1},{3,2},{4,3},{5,4},{6,5},{7,6},{8,15},{9,8},{10,9... | collective-permute-start | bytes 393224 | tf_op jit(solution)/shard_map/ppermute | solution.py:746
  116.4 4.9 %collective-permute-start.18 = (bf16[128,48]{1,0:T(8,128)(2,1)S(1)}, bf16[128,48]{1,0:T(8,128)(2,1)S(1)}, u32[]{:S(2)}, u32[]{:S(2)}) collective-permute-start(bf16[128,48]{1,0:T(8,128)(2,1)S(1)} %get-tuple-element.47), channel_id=1, source_target_pairs={{0,32},{32,64},{64,96},{96,0},{1,33},{33,65},{65,97},{97,1},{2,34}... | collective-permute-start | bytes 36872 | tf_op jit(solution)/shard_map/ppermute | solution.py:746
  117.9 3.4 %collective-permute-start.19 = (bf16[128,48]{1,0:T(8,128)(2,1)S(1)}, bf16[128,48]{1,0:T(8,128)(2,1)S(1)}, u32[]{:S(2)}, u32[]{:S(2)}) collective-permute-start(bf16[128,48]{1,0:T(8,128)(2,1)S(1)} %get-tuple-element.48), channel_id=1, source_target_pairs={{0,96},{32,0},{64,32},{96,64},{1,97},{33,1},{65,33},{97,65},{2,98}... | collective-permute-start | bytes 36872 | tf_op jit(solution)/shard_map/ppermute | solution.py:746
  121.3 3.8 %collective-permute-start.20 = (bf16[4,2,8,48]{3,2,1,0:T(8,128)(2,1)S(1)}, bf16[4,2,8,48]{3,2,1,0:T(8,128)(2,1)S(1)}, u32[]{:S(2)}, u32[]{:S(2)}) collective-permute-start(bf16[4,2,8,48]{3,2,1,0:T(8,128)(2,1)S(1)} %get-tuple-element.68), channel_id=1, source_target_pairs={{0,8},{8,16},{16,24},{24,0},{1,9},{9,17},{17,25},{25,1},{2,10},{10... | collective-permute-start | bytes 18440 | tf_op jit(solution)/shard_map/ppermute | solution.py:746
  121.7 4.9 %collective-permute-start.21 = (bf16[4,2,8,48]{3,2,1,0:T(8,128)(2,1)S(1)}, bf16[4,2,8,48]{3,2,1,0:T(8,128)(2,1)S(1)}, u32[]{:S(2)}, u32[]{:S(2)}) collective-permute-start(bf16[4,2,8,48]{3,2,1,0:T(8,128)(2,1)S(1)} %get-tuple-element.69), channel_id=1, source_target_pairs={{0,24},{8,0},{16,8},{24,16},{1,25},{9,1},{17,9},{25,17},{2,26},{10... | collective-permute-start | bytes 18440 | tf_op jit(solution)/shard_map/ppermute | solution.py:746
  126.7 5.8 %collective-permute-start.22 = (bf16[4,4,2,48]{3,2,1,0:T(2,128)(2,1)S(1)}, bf16[4,4,2,48]{3,2,1,0:T(2,128)(2,1)S(1)}, u32[]{:S(2)}, u32[]{:S(2)}) collective-permute-start(bf16[4,4,2,48]{3,2,1,0:T(2,128)(2,1)S(1)} %get-tuple-element.72), channel_id=1, source_target_pairs={{0,1},{1,2},{2,3},{3,4},{4,5},{5,6},{6,7},{7,0},{8,9},{9,10},{10,1... | collective-permute-start | bytes 9224 | tf_op jit(solution)/shard_map/ppermute | solution.py:746
  126.8 5.8 %collective-permute-start.23 = (bf16[4,4,2,48]{3,2,1,0:T(2,128)(2,1)S(1)}, bf16[4,4,2,48]{3,2,1,0:T(2,128)(2,1)S(1)}, u32[]{:S(2)}, u32[]{:S(2)}) collective-permute-start(bf16[4,4,2,48]{3,2,1,0:T(2,128)(2,1)S(1)} %get-tuple-element.73), channel_id=1, source_target_pairs={{0,7},{1,0},{2,1},{3,2},{4,3},{5,4},{6,5},{7,6},{8,15},{9,8},{10,9... | collective-permute-start | bytes 9224 | tf_op jit(solution)/shard_map/ppermute | solution.py:746
